TPU v7x, 128 devices: a whole 4x4x4 slice. The times are simulated.
128 devices in a mesh: dp: 2 (over core), expert: 64 (over z, y, x).
Axes of the slice: x: 4, y: 4, z: 4, core: 2. Of those that a mesh axis runs over, the one named last changes fastest.
Arguments:
- hidden: bfloat16 [32768, 2, 1024], P(('dp', 'expert')), may hold values from -0.75 to 0.75
- grad_out: bfloat16 [32768, 3584], P(('dp', 'expert')), may hold values from -6 to 6
- gates: bfloat16 [32768, 2], P(('dp', 'expert')), may hold values from 0.099609375 to 1
- expert_ids: int32 [32768, 2], P(('dp', 'expert')), may hold values from 0 to 63, all different within a row; in each aligned block of 256 rows (0 to 255, 256 to 511, ...) at most 10 rows name the same one
- weight: bfloat16 [64, 1024, 3584], P('expert', 'dp'), may hold values from -0.09375 to 0.09375
Outputs:
- grad_hidden: bfloat16 [32768, 2, 1024], P(('dp', 'expert'))
- grad_gates: float32 [32768, 2], P(('dp', 'expert'))
- weight_grad: bfloat16 [64, 1024, 3584], P('expert', 'dp')
Inputs may be any that keep to these rules, and one draw needn't show every extreme that they name: `expert_ids`: each token names 2 different experts; among the tokens of one device no expert is named more than 10 times, a bound that some block reaches.
All inputs are finite; a program needn't handle non-finite values.
Results may differ from a plain program's by a relative error of at most 0.0059.
Values may be sent and summed in bfloat16 or wider, within the bound.
No kernel may reach another device: no remote copies, remote signals or barrier semaphores. Data moves between devices by JAX's collectives and lax.ppermute only.
A program may use at most 128 MiB of HBM per device.

v0:
```python
import jax
import jax.numpy as jnp
from jax import lax
from jax.sharding import PartitionSpec as P


def per_device(hidden, grad_out, gates, expert_ids, weight):
    tokens_here, top_count, width_f = hidden.shape
    width_d = grad_out.shape[1]
    sources = lax.axis_size("expert")
    dp_groups = lax.axis_size("dp")
    experts = weight.shape[0] * sources
    capacity = max(2, 5 * top_count * tokens_here // (4 * experts))
    slots = experts * capacity
    contract_rows = (((0,), (0,)), ((), ()))
    contract_cols = (((1,), (1,)), ((), ()))
    routed = expert_ids.reshape(tokens_here * top_count)
    onehot = (routed[:, None] == jnp.arange(experts, dtype=jnp.int32)[None, :]).astype(jnp.int32)
    rank_in = jnp.sum((jnp.cumsum(onehot, axis=0) - 1) * onehot, axis=1)
    slot_index = routed * capacity + rank_in
    select = (slot_index[:, None] == jnp.arange(slots, dtype=jnp.int32)[None, :]).astype(
        jnp.bfloat16
    )
    token_select = jnp.sum(select.reshape(tokens_here, top_count, slots), axis=1)
    hidden_slots = lax.dot_general(
        select,
        hidden.reshape(tokens_here * top_count, width_f),
        contract_rows,
        preferred_element_type=jnp.float32,
    ).astype(jnp.bfloat16)
    grad_slots = lax.dot_general(
        token_select, grad_out, contract_rows, preferred_element_type=jnp.float32
    ).astype(jnp.bfloat16)
    gate_slots = jnp.sum(
        select.astype(jnp.float32) * gates.reshape(-1, 1).astype(jnp.float32), axis=0
    ).astype(jnp.bfloat16)
    received = (
        lax.all_to_all(
            hidden_slots.reshape(experts, capacity, width_f),
            "expert",
            split_axis=0,
            concat_axis=0,
            tiled=True,
        ),
        lax.all_to_all(
            grad_slots.reshape(experts, capacity, width_d),
            "expert",
            split_axis=0,
            concat_axis=0,
            tiled=True,
        ),
        lax.all_to_all(
            gate_slots.reshape(experts, capacity), "expert", split_axis=0, concat_axis=0, tiled=True
        ),
    )
    slot_rows = sources * capacity
    hidden_rows = received[0].reshape(slot_rows, width_f)
    grad_rows = received[1].reshape(slot_rows, width_d)
    gate_rows = received[2].reshape(slot_rows)
    scaled = (gate_rows.astype(jnp.float32)[:, None] * grad_rows.astype(jnp.float32)).astype(
        jnp.bfloat16
    )
    full_weight = lax.all_gather(weight[0], "dp", axis=0, tiled=True)
    raw_grad = lax.dot_general(
        grad_rows, full_weight, contract_cols, preferred_element_type=jnp.float32
    )
    partial_value = lax.dot_general(
        hidden_rows, scaled, contract_rows, preferred_element_type=jnp.float32
    )
    raw_rounded = raw_grad.astype(jnp.bfloat16)
    grad_pieces = partial_value.astype(jnp.bfloat16).reshape(
        dp_groups, width_f // dp_groups, width_d
    )
    collected = lax.all_to_all(grad_pieces, "dp", split_axis=0, concat_axis=0, tiled=True)
    weight_grad = jnp.sum(collected.astype(jnp.float32), axis=0).astype(jnp.bfloat16)[None]
    returned_rows = lax.all_to_all(
        raw_rounded.reshape(sources, capacity, width_f),
        "expert",
        split_axis=0,
        concat_axis=0,
        tiled=True,
    )
    raw_tok = jnp.dot(
        select, returned_rows.reshape(slots, width_f), preferred_element_type=jnp.float32
    )
    raw_tok = raw_tok.reshape(tokens_here, top_count, width_f)
    grad_hidden = (gates.astype(jnp.float32)[:, :, None] * raw_tok).astype(jnp.bfloat16)
    grad_gates = jnp.sum(hidden.astype(jnp.float32) * raw_tok, axis=2)
    return (grad_hidden, grad_gates, weight_grad)


def solution(mesh):
    in_specs = (
        P(("dp", "expert"), None, None),
        P(("dp", "expert"), None),
        P(("dp", "expert"), None),
        P(("dp", "expert"), None),
        P("expert", "dp", None),
    )
    out_specs = (
        P(("dp", "expert"), None, None),
        P(("dp", "expert"), None),
        P("expert", "dp", None),
    )
    return jax.shard_map(
        per_device, mesh=mesh, in_specs=in_specs, out_specs=out_specs, check_vma=False
    )
```

profile of v0, /device:TPU:0, one launch (start us, length us, event | category | flops | bytes accessed | tf_op | source)
XLA Modules:
  0.0 271.6 jit_solution(15490482061147586198)
XLA Ops:
  7.2 0.0 copy-start
  7.2 0.9 copy.49
  8.1 0.1 eq.67
  8.3 0.1 eq.71
  8.4 1.2 reduce-window.6
  9.7 0.2 slice_reduce_fusion
  9.9 0.8 copy.54
  10.7 0.1 reshape.139
  10.9 0.1 fusion.16
  11.0 0.3 multiply_reduce_fusion.1
  11.3 0.8 convert_element_type.103
  12.0 11.5 %all-to-all-start.3 = ((bf16[64,1,10]{2,1,0:T(2,128)(2,1)}), bf16[64,1,10]{2,1,0:T(2,128)(2,1)S(1)}, u32[]{:S(2)}, u32[]{:S(2)}) async-start(bf16[64,1,10]{2,1,0:T(2,128)(2,1)} %convert_element_type.103), calls=%async_computation.3 | async-start | bytes 65536 | tf_op jit(solution)/shard_map/all_to_all | solution.py:52
  23.5 0.1 reduce_sum.54
  23.7 0.1 copy.52
  23.8 0.7 multiply_add_fusion.1
  24.5 0.2 fusion.12
  24.7 0.0 copy-done
  24.7 3.4 %convolution_convert_fusion = bf16[640,3584]{1,0:T(8,128)(2,1)} fusion(bf16[256,640]{1,0:T(8,128)(2,1)S(1)} %fusion.12, bf16[256,3584]{1,0:T(8,128)(2,1)S(1)} %copy-done), kind=kOutput, calls=%fused_computation.4 | convolution fusion | flops 1176698880 | bytes 6750208 | tf_op jit(solution)/shard_map/dot_general | solution.py:31
  28.1 7.7 %reshape.132 = bf16[64,10,3584]{2,1,0:T(8,128)(2,1)} reshape(bf16[640,3584]{1,0:T(8,128)(2,1)} %convolution_convert_fusion) | data formatting | bytes 9175040 | tf_op jit(solution)/shard_map/reshape | solution.py:46
  35.8 0.0 all-to-all-done.3
  35.8 10.6 %all-to-all-start = ((bf16[64,10,3584]{2,1,0:T(8,128)(2,1)}), bf16[64,10,3584]{2,1,0:T(8,128)(2,1)}, u32[]{:S(2)}, u32[]{:S(2)}) async-start(bf16[64,10,3584]{2,1,0:T(8,128)(2,1)} %reshape.132), calls=%async_computation | async-start | bytes 14680064 | tf_op jit(solution)/shard_map/all_to_all | solution.py:45
  46.4 0.0 copy-start.2
  46.4 0.0 all-gather.3.cloned.1.call-start
  46.4 0.7 all-gather.3.cloned.1.call-update
  47.1 0.5 copy-done.2
  47.6 0.4 reshape.136
  48.0 1.0 convolution_convert_fusion.1
  49.0 1.5 reshape.137
  50.6 89.5 %all-to-all-done = bf16[64,10,3584]{2,1,0:T(8,128)(2,1)} async-done(((bf16[64,10,3584]{2,1,0:T(8,128)(2,1)}), bf16[64,10,3584]{2,1,0:T(8,128)(2,1)}, u32[]{:S(2)}, u32[]{:S(2)}) %all-to-all-start) | async-done | bytes 4587552 | tf_op jit(solution)/shard_map/all_to_all | solution.py:45
  140.1 13.8 %all-to-all-start.2 = ((bf16[64,10,1024]{2,1,0:T(8,128)(2,1)}), bf16[64,10,1024]{2,1,0:T(8,128)(2,1)}, u32[]{:S(2)}, u32[]{:S(2)}) async-start(bf16[64,10,1024]{2,1,0:T(8,128)(2,1)} %reshape.137), calls=%async_computation.2 | async-start | bytes 4194304 | tf_op jit(solution)/shard_map/all_to_all | solution.py:38
  153.9 8.6 %multiply_convert_fusion = bf16[64,10,3584]{2,1,0:T(8,128)(2,1)} fusion(bf16[64,10,3584]{2,1,0:T(8,128)(2,1)} %all-to-all-done, f32[64,10]{1,0:T(8,128)S(1)} %bitcast.37), kind=kLoop, calls=%fused_computation.1 | loop fusion | flops 6881280 | bytes 9177600 | tf_op jit(solution)/shard_map/convert_element_type | solution.py:60
  162.4 19.3 %all-to-all-done.2 = bf16[64,10,1024]{2,1,0:T(8,128)(2,1)} async-done(((bf16[64,10,1024]{2,1,0:T(8,128)(2,1)}), bf16[64,10,1024]{2,1,0:T(8,128)(2,1)}, u32[]{:S(2)}, u32[]{:S(2)}) %all-to-all-start.2) | async-done | bytes 1310752 | tf_op jit(solution)/shard_map/all_to_all | solution.py:38
  181.7 12.9 %bitcast_convert_fusion = bf16[1024,3584]{1,0:T(8,128)(2,1)} fusion(bf16[64,10,3584]{2,1,0:T(8,128)(2,1)} %multiply_convert_fusion, bf16[64,10,1024]{2,1,0:T(8,128)(2,1)} %all-to-all-done.2), kind=kOutput, calls=%fused_computation | convolution fusion | flops 4701290496 | bytes 13238272 | tf_op jit(solution)/shard_map/dot_general | solution.py:67
  194.6 6.7 %all-to-all-start.4 = ((bf16[2,512,3584]{2,1,0:T(8,128)(2,1)}), bf16[2,512,3584]{2,1,0:T(8,128)(2,1)}, u32[]{:S(2)}, u32[]{:S(2)}) async-start(bf16[2,512,3584]{2,1,0:T(8,128)(2,1)} %bitcast.35), calls=%async_computation.4 | async-start | bytes 14680064 | tf_op jit(solution)/shard_map/all_to_all | solution.py:74
  201.3 8.0 %reshape.133 = bf16[640,3584]{1,0:T(8,128)(2,1)} reshape(bf16[64,10,3584]{2,1,0:T(8,128)(2,1)} %all-to-all-done) | data formatting | bytes 9175040 | tf_op jit(solution)/shard_map/reshape | solution.py:58
  209.3 0.0 all-gather.3.cloned.1.call-done
  209.3 9.4 %fusion.3 = bf16[640,1024]{1,0:T(8,128)(2,1)S(1)} fusion(bf16[640,3584]{1,0:T(8,128)(2,1)} %reshape.133, bf16[1,1024,3584]{2,1,0:T(8,128)(2,1)} %all-gather.3.cloned.1.call-done), kind=kOutput, calls=%fused_computation.8 | convolution fusion | flops 4698275840 | bytes 13238272 | tf_op jit(solution)/shard_map/dot_general | solution.py:64
  218.7 1.6 reshape.134
  220.2 0.0 copy-start.3
  220.2 0.0 all-to-all-done.4
  220.2 6.0 %all-to-all-start.1 = ((bf16[64,10,1024]{2,1,0:T(8,128)(2,1)}), bf16[64,10,1024]{2,1,0:T(8,128)(2,1)}, u32[]{:S(2)}, u32[]{:S(2)}) async-start(bf16[64,10,1024]{2,1,0:T(8,128)(2,1)} %reshape.134), calls=%async_computation.1 | async-start | bytes 4194304 | tf_op jit(solution)/shard_map/all_to_all | solution.py:76
  226.2 0.0 copy-done.3
  226.3 7.3 %reduce_sum.58 = bf16[512,3584]{1,0:T(8,128)(2,1)} reduce(bf16[2,512,3584]{2,1,0:T(8,128)(2,1)} %all-to-all-done.4, bf16[]{:T(256)} %constant.14.clone.1), dimensions={0}, to_apply=%region_6.7 | reduce | flops 1835008 | bytes 11010050 | tf_op jit(solution)/shard_map/reduce_sum | solution.py:75
  233.5 23.4 %all-to-all-done.1 = bf16[64,10,1024]{2,1,0:T(8,128)(2,1)} async-done(((bf16[64,10,1024]{2,1,0:T(8,128)(2,1)}), bf16[64,10,1024]{2,1,0:T(8,128)(2,1)}, u32[]{:S(2)}, u32[]{:S(2)}) %all-to-all-start.1) | async-done | bytes 1310752 | tf_op jit(solution)/shard_map/all_to_all | solution.py:76
  256.9 2.6 reshape.142
  259.5 0.0 copy-start.1
  259.5 3.2 %multiply_reduce_fusion = (f32[256,2]{0,1:T(2,128)}, bf16[256,2,1024]{2,0,1:T(8,128)(2,1)S(1)}) fusion(bf16[256,2,1024]{2,1,0:T(2,128)(2,1)} %param.5, f32[256,2]{0,1:T(2,128)S(1)} %convert_element_type.82, bf16[640,1024,1]{1,0,2:T(8,128)(2,1)S(1)} %reshape.142, s32[256,2]{0,1:T(2,128)S(1)} %multiply_add_fusion.1), kind=kOutput, calls=%fused_computation.6 | convolution fusion | flops 674037248 | bytes 3414016 | tf_op jit(solution)/shard_map/dot_general | solution.py:83
  262.7 2.0 copy.58
  264.8 0.0 copy-done.1
  (6 shorter events, 0.1 us)
Async XLA Ops:
  7.2 17.5 %copy-start = (bf16[256,3584]{1,0:T(8,128)(2,1)S(1)}, bf16[256,3584]{1,0:T(8,128)(2,1)}, u32[]{:S(2)}) copy-start(bf16[256,3584]{1,0:T(8,128)(2,1)} %param.6) | copy-start | bytes 5505028
  12.0 23.7 %all-to-all-start.3 = ((bf16[64,1,10]{2,1,0:T(2,128)(2,1)}), bf16[64,1,10]{2,1,0:T(2,128)(2,1)S(1)}, u32[]{:S(2)}, u32[]{:S(2)}) async-start(bf16[64,1,10]{2,1,0:T(2,128)(2,1)} %convert_element_type.103), calls=%async_computation.3 | async-start | bytes 65536 | tf_op jit(solution)/shard_map/all_to_all | solution.py:52
  35.8 104.3 %all-to-all-start = ((bf16[64,10,3584]{2,1,0:T(8,128)(2,1)}), bf16[64,10,3584]{2,1,0:T(8,128)(2,1)}, u32[]{:S(2)}, u32[]{:S(2)}) async-start(bf16[64,10,3584]{2,1,0:T(8,128)(2,1)} %reshape.132), calls=%async_computation | async-start | bytes 14680064 | tf_op jit(solution)/shard_map/all_to_all | solution.py:45
  46.4 1.2 copy-start.2
  46.4 162.9 %all-gather.3.cloned.1.call-start = ((), (), s32[]{:S(2)}) async-start(), calls=%async_computation.5 | async-start | bytes 11010048 | tf_op jit(solution)/shard_map/all_gather | solution.py:63
  140.1 41.6 %all-to-all-start.2 = ((bf16[64,10,1024]{2,1,0:T(8,128)(2,1)}), bf16[64,10,1024]{2,1,0:T(8,128)(2,1)}, u32[]{:S(2)}, u32[]{:S(2)}) async-start(bf16[64,10,1024]{2,1,0:T(8,128)(2,1)} %reshape.137), calls=%async_computation.2 | async-start | bytes 4194304 | tf_op jit(solution)/shard_map/all_to_all | solution.py:38
  194.6 25.6 %all-to-all-start.4 = ((bf16[2,512,3584]{2,1,0:T(8,128)(2,1)}), bf16[2,512,3584]{2,1,0:T(8,128)(2,1)}, u32[]{:S(2)}, u32[]{:S(2)}) async-start(bf16[2,512,3584]{2,1,0:T(8,128)(2,1)} %bitcast.35), calls=%async_computation.4 | async-start | bytes 14680064 | tf_op jit(solution)/shard_map/all_to_all | solution.py:74
  220.2 6.0 %copy-start.3 = (bf16[256,2]{0,1:T(2,128)(2,1)S(1)}, bf16[256,2]{0,1:T(2,128)(2,1)}, u32[]{:S(2)}) copy-start(bf16[256,2]{0,1:T(2,128)(2,1)} %param.7) | copy-start | bytes 3076
  220.2 36.7 %all-to-all-start.1 = ((bf16[64,10,1024]{2,1,0:T(8,128)(2,1)}), bf16[64,10,1024]{2,1,0:T(8,128)(2,1)}, u32[]{:S(2)}, u32[]{:S(2)}) async-start(bf16[64,10,1024]{2,1,0:T(8,128)(2,1)} %reshape.134), calls=%async_computation.1 | async-start | bytes 4194304 | tf_op jit(solution)/shard_map/all_to_all | solution.py:76
  259.5 5.2 %copy-start.1 = (bf16[256,3584]{1,0:T(8,128)(2,1)S(1)}, bf16[256,3584]{1,0:T(8,128)(2,1)}, u32[]{:S(2)}) copy-start(bf16[256,3584]{1,0:T(8,128)(2,1)} %param.6) | copy-start | bytes 5505028
Sparse Core Ops, SparseCore 0:
  48.9 22.2 all-gather.2
where the time goes:
time: 273 us; the launch traced here: 272 us
  waiting for transfers between devices  133 us (49%)
  starting transfers between devices  48.5 us (18%)
  matrix products  29.9 us (11%)
  local copies, waits for them, and re-layouts  27.7 us (10%)
  other arithmetic  18.4 us (7%)
  between operations  14.2 us (5%)
    all_to_all x1, waiting for transfers between devices, per_device(): lax.all_to_all(grad_slots.reshape(experts, capacity, width_d), 'expert',...  89.5 us
    all_to_all x1, waiting for transfers between devices, per_device(): lax.all_to_all(raw_rounded.reshape(sources, capacity, width_f), 'expert',...  23.4 us
    all_to_all x1, waiting for transfers between devices, per_device(): lax.all_to_all(hidden_slots.reshape(experts, capacity, width_f), 'expert'...  19.3 us
    all_to_all x1, starting transfers between devices, per_device(): lax.all_to_all(hidden_slots.reshape(experts, capacity, width_f), 'expert'...  13.8 us
    dot_general x1, matrix products, per_device(): lax.dot_general(hidden_rows, scaled, contract_rows, preferred_element_typ...  12.9 us
    all_to_all x1, starting transfers between devices, per_device(): lax.all_to_all(gate_slots.reshape(experts, capacity), 'expert', split_axi...  11.5 us
    all_to_all x1, starting transfers between devices, per_device(): lax.all_to_all(grad_slots.reshape(experts, capacity, width_d), 'expert',...  10.6 us
    dot_general x1, matrix products, per_device(): lax.dot_general(grad_rows, full_weight, contract_cols, preferred_element_...  9.4 us
  transfers between devices with their start and end apart: 6, of which 3 were waited for; matrix products, arithmetic and copies ran while one was open for 23% of the time, Pallas kernels for 0%

commit v1 on v0

v1 whole, which is shorter than its diff:
```python
import functools

import jax
import jax.numpy as jnp
from jax import lax
from jax.experimental import pallas as pl
from jax.experimental.pallas import tpu as pltpu
from jax.sharding import PartitionSpec as P

T = 256
A = 512
E = 64
D = 3584
F = 1024
COL = 512
FOLD = COL // 4
BLK = COL + FOLD
NG = D // COL
NH = F // COL
MSG = BLK * (NG + NH)
RET = F + F // 4
ROWS = 512
OVER = 128
BF = jnp.bfloat16
F32 = jnp.float32
VMEM = 56 * 1024 * 1024


def iota(shape, axis):
    return lax.broadcasted_iota(jnp.int32, shape, axis)


def dot(a, b):
    return jnp.dot(a, b, preferred_element_type=F32)


def dot_nt(a, b):
    return lax.dot_general(a, b, (((1,), (1,)), ((), ())), preferred_element_type=F32)


def rank_maps(ids):
    experts = iota((E, T), 0)
    o0 = (ids[0:1, :] == experts).astype(F32)
    o1 = (ids[1:2, :] == experts).astype(F32)
    earlier = (iota((T, T), 0) < iota((T, T), 1)).astype(BF)
    count = dot((o0 + o1).astype(BF), earlier)
    return (o0 * (count + 1.0)).astype(BF), (o1 * (count + 1.0)).astype(BF)


def interleave(k):
    return (iota((T, A), 1) == 2 * iota((T, A), 0) + k).astype(BF)


def spread():
    return (jnp.right_shift(iota((ROWS, E), 0), 3) == iota((ROWS, E), 1)).astype(BF)


def pack_kernel(ids_ref, gates_ref, grad_ref, hid_ref, out_ref, sm, sf, hm, hf):
    j = pl.program_id(0)

    @pl.when(j == 0)
    def _():
        r0, r1 = rank_maps(ids_ref[...])
        rows = spread()
        by_token = dot(rows, (r0.astype(F32) + r1.astype(F32)).astype(BF)).astype(jnp.int32)
        row = iota((ROWS, T), 0)
        sm[...] = (by_token == (row & 7) + 1).astype(F32).astype(BF)
        over = by_token == (row & 1) + 9
        quarter = jnp.right_shift(row, 1) & 3
        for q in range(4):
            sf[:, q * T : (q + 1) * T] = (over & (quarter == q)).astype(F32).astype(BF)
        p0, p1 = interleave(0), interleave(1)
        by_assign = dot(rows, (dot(r0, p0) + dot(r1, p1)).astype(BF)).astype(jnp.int32)
        gates = gates_ref[...]
        gate = dot(gates, p0)[0:1, :] + dot(gates, p1)[1:2, :]
        row = iota((ROWS, A), 0)
        hm[...] = jnp.where(by_assign == (row & 7) + 1, gate, 0.0).astype(BF)
        over = by_assign == (row & 1) + 9
        quarter = jnp.right_shift(row, 1) & 3
        for q in range(4):
            hf[:, q * A : (q + 1) * A] = jnp.where(over & (quarter == q), gate, 0.0).astype(BF)

    def emit(main_sel, fold_sel, x):
        out_ref[:, :COL] = dot(main_sel[...], x).astype(BF)
        stacked = jnp.concatenate([x[:, q * FOLD : (q + 1) * FOLD] for q in range(4)], axis=0)
        out_ref[:, COL:] = dot(fold_sel[...], stacked).astype(BF)

    @pl.when(j < NG)
    def _():
        emit(sm, sf, grad_ref[...])

    @pl.when(j >= NG)
    def _():
        emit(hm, hf, hid_ref[...])


def pack(ids, gates, grad, hid):
    return pl.pallas_call(
        pack_kernel,
        grid=(NG + NH,),
        in_specs=[
            pl.BlockSpec((2, T), lambda j: (0, 0)),
            pl.BlockSpec((2, T), lambda j: (0, 0)),
            pl.BlockSpec((T, COL), lambda j: (0, jnp.minimum(j, NG - 1))),
            pl.BlockSpec((A, COL), lambda j: (0, jnp.maximum(j - NG, 0))),
        ],
        out_specs=pl.BlockSpec((ROWS, BLK), lambda j: (0, j)),
        out_shape=jax.ShapeDtypeStruct((ROWS, MSG), BF),
        scratch_shapes=[
            pltpu.VMEM((ROWS, T), BF),
            pltpu.VMEM((ROWS, 4 * T), BF),
            pltpu.VMEM((ROWS, A), BF),
            pltpu.VMEM((ROWS, 4 * A), BF),
        ],
        compiler_params=pltpu.CompilerParams(vmem_limit_bytes=VMEM),
        name="pack",
    )(ids, gates, grad, hid)


def select_kernel(ids_ref, main_ref, fold_ref):
    r0, r1 = rank_maps(ids_ref[...])
    by_assign = dot(spread(), (dot(r0, interleave(0)) + dot(r1, interleave(1))).astype(BF))
    by_assign = by_assign.T.astype(jnp.int32)
    row = iota((A, ROWS), 1)
    main_ref[...] = (by_assign == (row & 7) + 1).astype(F32).astype(BF)
    fold_ref[...] = (by_assign == (row & 1) + 9).astype(F32).astype(BF)


def select(ids):
    shape = jax.ShapeDtypeStruct((A, ROWS), BF)
    return pl.pallas_call(
        select_kernel,
        out_shape=(shape, shape),
        compiler_params=pltpu.CompilerParams(vmem_limit_bytes=VMEM),
        name="select",
    )(ids)


def unfold_matrix():
    i, j = iota((ROWS, ROWS), 0), iota((ROWS, ROWS), 1)
    home = jnp.right_shift(i & 127, 1) * 8 + jnp.right_shift(i, 7) * 2 + (i & 1)
    return (home == j).astype(F32).astype(BF)


def fold_matrix():
    j, i = iota((ROWS, ROWS), 0), iota((ROWS, ROWS), 1)
    home = jnp.right_shift(i & 127, 1) * 8 + jnp.right_shift(i, 7) * 2 + (i & 1)
    return (home == j).astype(F32).astype(BF)


def unfold(matrix, folded):
    rows = dot(matrix, folded).astype(BF)
    return jnp.concatenate([rows[q * OVER : (q + 1) * OVER, :] for q in range(4)], axis=1)


def raw_kernel(msg_ref, w_ref, out_ref, acc, um):
    j = pl.program_id(0)

    @pl.when(j == 0)
    def _():
        um[...] = unfold_matrix()
        acc[...] = jnp.zeros_like(acc)

    w = w_ref[...]
    acc[:ROWS, :] += dot_nt(msg_ref[:, :COL], w)
    acc[ROWS:, :] += dot_nt(unfold(um[...], msg_ref[:, COL:]), w)

    @pl.when(j == NG - 1)
    def _():
        out_ref[:, :F] = acc[:ROWS, :].astype(BF)
        over = acc[ROWS:, :].astype(BF)
        stacked = jnp.concatenate([over[:, q * 256 : (q + 1) * 256] for q in range(4)], axis=0)
        out_ref[:, F:] = dot(fold_matrix(), stacked).astype(BF)


def raw_rows(msg, weight):
    return pl.pallas_call(
        raw_kernel,
        grid=(NG,),
        in_specs=[
            pl.BlockSpec((ROWS, BLK), lambda j: (0, j)),
            pl.BlockSpec((F, COL), lambda j: (0, j)),
        ],
        out_specs=pl.BlockSpec((ROWS, RET), lambda j: (0, 0)),
        out_shape=jax.ShapeDtypeStruct((ROWS, RET), BF),
        scratch_shapes=[pltpu.VMEM((ROWS + OVER, F), F32), pltpu.VMEM((ROWS, ROWS), BF)],
        compiler_params=pltpu.CompilerParams(vmem_limit_bytes=VMEM),
        name="raw",
    )(msg, weight)


def partial_kernel(add, half_ref, msg_ref, hid_ref, *rest):
    if add:
        got_ref, out_ref, ht, um = rest
    else:
        out_ref, ht, um = rest
    j = pl.program_id(0)

    @pl.when(j == 0)
    def _():
        um[...] = unfold_matrix()
        ht[:, :ROWS] = hid_ref[:, :COL].T
        ht[:, ROWS:] = unfold(um[...], hid_ref[:, COL:]).T

    value = dot(ht[:, :ROWS], msg_ref[:, :COL])
    value += dot(ht[:, ROWS:], unfold(um[...], msg_ref[:, COL:]))
    if add:
        value = value.astype(BF).astype(F32) + got_ref[...].astype(F32)
    out_ref[...] = value.astype(BF)


def partial_half(half, msg, got=None):
    in_specs = [
        pl.BlockSpec((ROWS, BLK), lambda j, half: (0, j)),
        pl.BlockSpec((ROWS, BLK), lambda j, half: (0, NG + half[0])),
    ]
    args = [half, msg, msg]
    block = pl.BlockSpec((COL, COL), lambda j, half: (0, j))
    if got is not None:
        in_specs.append(block)
        args.append(got)
    return pl.pallas_call(
        functools.partial(partial_kernel, got is not None),
        grid_spec=pltpu.PrefetchScalarGridSpec(
            num_scalar_prefetch=1,
            grid=(NG,),
            in_specs=in_specs,
            out_specs=block,
            scratch_shapes=[
                pltpu.VMEM((COL, ROWS + OVER), BF),
                pltpu.VMEM((ROWS, ROWS), BF),
            ],
        ),
        out_shape=jax.ShapeDtypeStruct((COL, D), BF),
        compiler_params=pltpu.CompilerParams(vmem_limit_bytes=VMEM),
        name="partial_own" if got is not None else "partial_other",
    )(*args)


def combine_kernel(main_ref, fold_ref, ret_ref, gate_ref, hid_ref, out_ref, gg_ref):
    folded = ret_ref[:, F:]
    pick = fold_ref[...]
    quarter = jnp.right_shift(iota((1, ROWS), 1), 1) & 3
    gate = gate_ref[...].astype(F32)
    total = jnp.zeros((A, 1), F32)
    for q in range(4):
        cols = slice(q * 256, (q + 1) * 256)
        raw = dot(main_ref[...], ret_ref[:, cols])
        raw += dot(pick * (quarter == q).astype(F32).astype(BF), folded)
        out_ref[:, cols] = (gate * raw).astype(BF)
        total += jnp.sum(hid_ref[:, cols].astype(F32) * raw, axis=1, keepdims=True)
    gg_ref[...] = total


def combine(main_sel, fold_sel, ret, gate, hid):
    return pl.pallas_call(
        combine_kernel,
        out_shape=(jax.ShapeDtypeStruct((A, F), BF), jax.ShapeDtypeStruct((A, 1), F32)),
        compiler_params=pltpu.CompilerParams(vmem_limit_bytes=VMEM),
        name="combine",
    )(main_sel, fold_sel, ret, gate, hid)


def exchange(x):
    width = x.shape[1]
    swapped = lax.all_to_all(
        x.reshape(E, 8, width), "expert", split_axis=0, concat_axis=0, tiled=True
    )
    return swapped.reshape(ROWS, width)


def per_device(hidden, grad_out, gates, expert_ids, weight):
    dp = lax.axis_index("dp").astype(jnp.int32)
    ids = expert_ids.T
    hid = hidden.reshape(A, F)
    msg = exchange(pack(ids, gates.T, grad_out, hid))
    full_weight = lax.all_gather(weight[0], "dp", axis=0, tiled=True)
    main_sel, fold_sel = select(ids)
    ret = exchange(raw_rows(msg, full_weight))
    sent = partial_half((1 - dp).reshape(1), msg)
    got = lax.ppermute(sent, "dp", [(0, 1), (1, 0)])
    weight_grad = partial_half(dp.reshape(1), msg, got)
    grad_hidden, grad_gates = combine(main_sel, fold_sel, ret, gates.reshape(A, 1), hid)
    return grad_hidden.reshape(T, 2, F), grad_gates.reshape(T, 2), weight_grad[None]


def solution(mesh):
    in_specs = (
        P(("dp", "expert"), None, None),
        P(("dp", "expert"), None),
        P(("dp", "expert"), None),
        P(("dp", "expert"), None),
        P("expert", "dp", None),
    )
    out_specs = (
        P(("dp", "expert"), None, None),
        P(("dp", "expert"), None),
        P("expert", "dp", None),
    )
    return jax.shard_map(
        per_device, mesh=mesh, in_specs=in_specs, out_specs=out_specs, check_vma=False
    )
```

time: 273 us -> 196 us (0.72)
  Pallas kernels: 0 us -> 54.4 us
  waiting for transfers between devices: 133 us -> 94.3 us
  matrix products: 29.9 us -> 0 us
  starting transfers between devices: 48.5 us -> 24.1 us
  local copies, waits for them, and re-layouts: 27.7 us -> 7.29 us
  other arithmetic: 18.4 us -> 1.09 us
    pallas_call x0 -> x6, Pallas kernels: none -> 54.4 us  [the longest x2 22.2 us: partial_half(): pl.pallas_call(functools.partial(partial_kernel, got is not None), grid_s...]
    all_to_all x5 -> x2, waiting for transfers between devices: 132 us -> 93.6 us  [exchange(): lax.all_to_all(x.reshape(E, 8, width), 'expert', split_axis=0, concat_axi...]
    dot_general x5 -> x0, matrix products: 29.9 us -> none  [the longest x1 12.9 us: per_device(): lax.dot_general(hidden_rows, scaled, contract_rows, preferred_element_typ...]
    all_to_all x5 -> x2, starting transfers between devices: 48.5 us -> 24.1 us  [exchange(): lax.all_to_all(x.reshape(E, 8, width), 'expert', split_axis=0, concat_axi...]
    reshape x6 -> x4, local copies, waits for them, and re-layouts: 21.7 us -> 5.4 us  [the longest x1 2.25 us: per_device(): hid = hidden.reshape(A, F)]
    convert_element_type x4 -> x0, other arithmetic: 8.62 us -> none  [the longest x1 8.57 us: per_device(): (gate_rows.astype(jnp.float32)[:, None] * grad_rows.astype(jnp.float32))....]
    reduce_sum x4 -> x0, other arithmetic: 7.83 us -> none  [the longest x1 7.28 us: per_device(): jnp.sum(collected.astype(jnp.float32), axis=0).astype(jnp.bfloat16)[None]]
  transfers between devices with their start and end apart: 6 -> 4, of which waited for: 3 -> 2; matrix products, arithmetic and copies ran while one was open for 23% -> 3% of each run, Pallas kernels for 0% -> 16%
where the time goes in v1:
time: 196 us; the launch traced here: 195 us
  waiting for transfers between devices  94.3 us (48%)
  Pallas kernels  54.4 us (28%)
  starting transfers between devices  24.1 us (12%)
  between operations  14.1 us (7%)
  local copies, waits for them, and re-layouts  7.29 us (4%)
    all_to_all x2, waiting for transfers between devices, exchange(): lax.all_to_all(x.reshape(E, 8, width), 'expert', split_axis=0, concat_axi...  93.6 us
    all_to_all x2, starting transfers between devices, exchange(): lax.all_to_all(x.reshape(E, 8, width), 'expert', split_axis=0, concat_axi...  24.1 us
    pallas_call x2, Pallas kernels, partial_half(): pl.pallas_call(functools.partial(partial_kernel, got is not None), grid_s...  22.2 us
    pallas_call x1, Pallas kernels, raw_rows(): pl.pallas_call(raw_kernel, grid=(NG,), in_specs=[pl.BlockSpec((ROWS, BLK)...  13.3 us
    pallas_call x1, Pallas kernels, pack(): pl.pallas_call(pack_kernel, grid=(NG + NH,), in_specs=[pl.BlockSpec((2, T...  12 us
    pallas_call x1, Pallas kernels, combine(): pl.pallas_call(combine_kernel, out_shape=(jax.ShapeDtypeStruct((A, F), BF...  4.32 us
  transfers between devices with their start and end apart: 4, of which 2 were waited for; matrix products, arithmetic and copies ran while one was open for 3% of the time, Pallas kernels for 16%

profile of v1, /device:TPU:0, one launch (start us, length us, event | category | flops | bytes accessed | tf_op | source)
XLA Modules:
  0.0 195.3 jit_solution(18065441667445558477)
XLA Ops:
  7.2 2.3 %reshape.36.hid_ref = bf16[512,1024]{1,0:T(8,128)(2,1)} reshape(bf16[256,2,1024]{2,1,0:T(2,128)(2,1)} %param.5) | data formatting | bytes 2097152 | tf_op jit(solution)/shard_map/reshape | solution.py:275
  9.4 12.0 %pack.1 = bf16[512,5760]{1,0:T(8,128)(2,1)} custom-call(s32[2,256]{1,0:T(2,128)} %bitcast.15, bf16[2,256]{1,0:T(2,128)(2,1)} %bitcast.17, bf16[256,3584]{1,0:T(8,128)(2,1)} %grad_ref.1, bf16[512,1024]{1,0:T(8,128)(2,1)} %reshape.36.hid_ref), custom_call_target="tpu_custom_call" | custom-call | tf_op jit(solution)/shard_map/pack/pallas_call | solution.py:98
  21.5 11.7 %all-to-all-start = ((bf16[64,8,5760]{2,1,0:T(8,128)(2,1)}), bf16[64,8,5760]{2,1,0:T(8,128)(2,1)}, u32[]{:S(2)}, u32[]{:S(2)}) async-start(bf16[64,8,5760]{2,1,0:T(8,128)(2,1)} %bitcast.10), calls=%async_computation | async-start | bytes 11796480 | tf_op jit(solution)/shard_map/all_to_all | solution.py:266
  33.2 0.0 all-gather.3.cloned.1.call-start
  33.2 0.7 all-gather.3.cloned.1.call-update
  33.9 74.7 %all-to-all-done = bf16[64,8,5760]{2,1,0:T(8,128)(2,1)} async-done(((bf16[64,8,5760]{2,1,0:T(8,128)(2,1)}), bf16[64,8,5760]{2,1,0:T(8,128)(2,1)}, u32[]{:S(2)}, u32[]{:S(2)}) %all-to-all-start) | async-done | bytes 5898272 | tf_op jit(solution)/shard_map/all_to_all | solution.py:266
  108.7 10.7 %partial_other.1 = bf16[512,3584]{1,0:T(8,128)(2,1)} custom-call(s32[1]{0:T(128)} %bitcast.8.half_ref, bf16[512,5760]{1,0:T(8,128)(2,1)} %bitcast.3.msg_ref.hid_ref, bf16[512,5760]{1,0:T(8,128)(2,1)} %bitcast.3.msg_ref.hid_ref), custom_call_target="tpu_custom_call" | custom-call | tf_op jit(solution)/shard_map/partial_other/pallas_call | solution.py:222
  119.4 0.0 collective-permute-start
  119.4 0.0 all-gather.3.cloned.1.call-done
  119.4 0.0 copy-start.1
  119.4 13.3 %raw.1 = bf16[512,1280]{1,0:T(8,128)(2,1)} custom-call(bf16[512,5760]{1,0:T(8,128)(2,1)} %bitcast.3.msg_ref.hid_ref, bf16[1024,3584]{1,0:T(8,128)(2,1)} %bitcast.11), custom_call_target="tpu_custom_call" | custom-call | tf_op jit(solution)/shard_map/raw/pallas_call | solution.py:177
  132.8 12.4 %all-to-all-start.1 = ((bf16[64,8,1280]{2,1,0:T(8,128)(2,1)}), bf16[64,8,1280]{2,1,0:T(8,128)(2,1)S(1)}, u32[]{:S(2)}, u32[]{:S(2)}) async-start(bf16[64,8,1280]{2,1,0:T(8,128)(2,1)} %bitcast.13), calls=%async_computation.1 | async-start | bytes 2621440 | tf_op jit(solution)/shard_map/all_to_all | solution.py:266
  145.1 2.5 %select.1 = (bf16[512,512]{1,0:T(8,128)(2,1)}, bf16[512,512]{1,0:T(8,128)(2,1)}) custom-call(s32[2,256]{1,0:T(2,128)} %bitcast.16), custom_call_target="tpu_custom_call" | custom-call | tf_op jit(solution)/shard_map/select/pallas_call | solution.py:131
  147.7 0.0 copy-done.1
  147.7 0.1 copy.10
  147.8 0.8 reshape.47.gate_ref
  148.6 18.9 %all-to-all-done.1 = bf16[64,8,1280]{2,1,0:T(8,128)(2,1)S(1)} async-done(((bf16[64,8,1280]{2,1,0:T(8,128)(2,1)}), bf16[64,8,1280]{2,1,0:T(8,128)(2,1)S(1)}, u32[]{:S(2)}, u32[]{:S(2)}) %all-to-all-start.1) | async-done | bytes 1310752 | tf_op jit(solution)/shard_map/all_to_all | solution.py:266
  167.5 0.0 copy-start
  167.5 1.1 copy-done
  168.6 4.3 %combine.1 = (bf16[512,1024]{1,0:T(8,128)(2,1)}, f32[512,1]{1,0:T(8,128)}) custom-call(bf16[512,512]{1,0:T(8,128)(2,1)} %get-tuple-element.7.main_ref, bf16[512,512]{1,0:T(8,128)(2,1)} %get-tuple-element.8.fold_ref, bf16[512,1280]{1,0:T(8,128)(2,1)} %bitcast.12, bf16[512,1]{1,0:T(8,128)(2,1)} %reshape.47.gate_ref, bf16[512,1024]{1,0:T(8,128)(2,1)} %reshape.36.hid_ref), custom_call_target="tpu_custom_call" | custom-call | tf_op jit(solution)/shard_map/combine/pallas_call | solution.py:256
  172.9 2.2 %reshape.42 = bf16[256,2,1024]{2,1,0:T(2,128)(2,1)} reshape(bf16[512,1024]{1,0:T(8,128)(2,1)} %get-tuple-element.9) | data formatting | bytes 2097152 | tf_op jit(solution)/shard_map/reshape | solution.py:284
  175.1 1.1 reduce
  176.2 0.1 reshape.43
  176.4 0.7 copy.12
  177.0 0.0 collective-permute-done.rest_0_
  177.0 11.4 %partial_own.1 = bf16[512,3584]{1,0:T(8,128)(2,1)} custom-call(s32[1]{0:T(128)} %bitcast.7.half_ref, bf16[512,5760]{1,0:T(8,128)(2,1)} %bitcast.3.msg_ref.hid_ref, bf16[512,5760]{1,0:T(8,128)(2,1)} %bitcast.3.msg_ref.hid_ref, bf16[512,3584]{1,0:T(8,128)(2,1)} %collective-permute-done.rest_0_), custom_call_target="tpu_custom_call" | custom-call | tf_op jit(solution)/shard_map/partial_own/pallas_call | solution.py:222
Async XLA Ops:
  21.5 87.2 %all-to-all-start = ((bf16[64,8,5760]{2,1,0:T(8,128)(2,1)}), bf16[64,8,5760]{2,1,0:T(8,128)(2,1)}, u32[]{:S(2)}, u32[]{:S(2)}) async-start(bf16[64,8,5760]{2,1,0:T(8,128)(2,1)} %bitcast.10), calls=%async_computation | async-start | bytes 11796480 | tf_op jit(solution)/shard_map/all_to_all | solution.py:266
  33.2 86.2 %all-gather.3.cloned.1.call-start = ((), (), s32[]{:S(2)}) async-start(), calls=%async_computation.2 | async-start | bytes 11010048 | tf_op jit(solution)/shard_map/all_gather | solution.py:277
  119.4 57.6 %collective-permute-start = (bf16[512,3584]{1,0:T(8,128)(2,1)}, bf16[512,3584]{1,0:T(8,128)(2,1)}, u32[]{:S(2)}, u32[]{:S(2)}) collective-permute-start(bf16[512,3584]{1,0:T(8,128)(2,1)} %partial_other.1), channel_id=1, source_target_pairs={{0,64},{64,0},{1,65},{65,1},{2,66},{66,2},{3,67},{67,3},{4,68},{68... | collective-permute-start | bytes 11010056 | tf_op jit(solution)/shard_map/ppermute | solution.py:281
  119.4 28.3 %copy-start.1 = (bf16[256,2]{0,1:T(2,128)(2,1)S(1)}, bf16[256,2]{0,1:T(2,128)(2,1)}, u32[]{:S(2)}) copy-start(bf16[256,2]{0,1:T(2,128)(2,1)} %param.7) | copy-start | bytes 3076
  132.8 34.7 %all-to-all-start.1 = ((bf16[64,8,1280]{2,1,0:T(8,128)(2,1)}), bf16[64,8,1280]{2,1,0:T(8,128)(2,1)S(1)}, u32[]{:S(2)}, u32[]{:S(2)}) async-start(bf16[64,8,1280]{2,1,0:T(8,128)(2,1)} %bitcast.13), calls=%async_computation.1 | async-start | bytes 2621440 | tf_op jit(solution)/shard_map/all_to_all | solution.py:266
  167.5 1.1 copy-start
Sparse Core Ops, SparseCore 0:
  35.7 22.2 all-gather.2

commit v2 on v0

v2 whole, which is shorter than its diff:
```python
import jax
import jax.numpy as jnp
from jax import lax
from jax.experimental import pallas as pl
from jax.experimental.pallas import tpu as pltpu
from jax.sharding import PartitionSpec as P

T = 256
A = 512
E = 64
D = 3584
F = 1024
COL = 512
FOLD = COL // 4
BLK = COL + FOLD
NG = D // COL
NH = F // COL
MSG = BLK * (NG + NH)
RET = F + F // 4
ROWS = 512
OVER = 128
HALF = 256
BF = jnp.bfloat16
F32 = jnp.float32
PARAMS = pltpu.CompilerParams(vmem_limit_bytes=56 * 1024 * 1024)
ANY = pl.BlockSpec(memory_space=pl.ANY)
IN_VMEM = pl.BlockSpec(memory_space=pltpu.VMEM)
IN_SMEM = pl.BlockSpec(memory_space=pltpu.SMEM)


def iota(shape, axis):
    return lax.broadcasted_iota(jnp.int32, shape, axis)


def dot(a, b):
    return jnp.dot(a, b, preferred_element_type=F32)


def dot_nt(a, b):
    return lax.dot_general(a, b, (((1,), (1,)), ((), ())), preferred_element_type=F32)


def columns(j, width=COL):
    return slice(j * width, (j + 1) * width)


def main_cols(j):
    return slice(j * BLK, j * BLK + COL)


def fold_cols(j):
    return slice(j * BLK + COL, (j + 1) * BLK)


def fold_home(i):
    return jnp.right_shift(i & 63, 1) * 8 + jnp.right_shift(i, 6) * 2 + (i & 1)


def unfold_matrix():
    i, j = iota((HALF, HALF), 0), iota((HALF, HALF), 1)
    return (fold_home(i) == j).astype(F32).astype(BF)


def fold_matrix():
    j, i = iota((HALF, HALF), 0), iota((HALF, HALF), 1)
    return (fold_home(i) == j).astype(F32).astype(BF)


def unfold(matrix, folded):
    out = []
    for b in range(2):
        rows = dot(matrix, folded[columns(b, HALF), :]).astype(BF)
        out.append(jnp.concatenate([rows[columns(q, 64), :] for q in range(4)], axis=1))
    return jnp.concatenate(out, axis=0)


def fold(matrix, over):
    out = []
    width = over.shape[1] // 4
    for b in range(2):
        part = over[columns(b, 64), :]
        stacked = jnp.concatenate([part[:, columns(q, width)] for q in range(4)], axis=0)
        out.append(dot(matrix, stacked).astype(BF))
    return jnp.concatenate(out, axis=0)


def rank_maps(ids):
    experts = iota((E, T), 0)
    o0 = (ids[0:1, :] == experts).astype(F32)
    o1 = (ids[1:2, :] == experts).astype(F32)
    earlier = (iota((T, T), 0) < iota((T, T), 1)).astype(F32).astype(BF)
    count = dot((o0 + o1).astype(BF), earlier)
    return o0 * (count + 1.0), o1 * (count + 1.0)


def slots():
    i = iota((ROWS + OVER, 1), 0)
    main = i < ROWS
    expert = jnp.where(main, jnp.right_shift(i, 3), jnp.right_shift(i - ROWS, 1))
    rank = jnp.where(main, (i & 7) + 1, (i & 1) + 9)
    rows = (expert == iota((ROWS + OVER, E), 1)).astype(F32).astype(BF)
    return rows, rank.astype(F32)


def interleave(k):
    return (iota((T, A), 1) == 2 * iota((T, A), 0) + k).astype(F32).astype(BF)


def assignments(r0, r1):
    by_assign = dot(r0.astype(BF), interleave(0)) + dot(r1.astype(BF), interleave(1))
    return by_assign.astype(BF)


def pack_kernel(ids_ref, gates_ref, grad_ref, hid_ref, out_ref, grad, hid, out, sem, osem):
    copies = []
    for j in range(NG):
        copy = pltpu.make_async_copy(
            grad_ref.at[:, columns(j)], grad.at[:, columns(j)], sem.at[j]
        )
        copy.start()
        copies.append(copy)
    hid_copy = pltpu.make_async_copy(hid_ref, hid, sem.at[NG])
    hid_copy.start()
    r0, r1 = rank_maps(ids_ref[...])
    rows, rank = slots()
    sel = (dot(rows, (r0 + r1).astype(BF)) == rank).astype(F32).astype(BF)
    matrix = fold_matrix()
    outs = []

    def emit(j, chosen, x):
        value = dot(chosen, x)
        out[:, main_cols(j)] = value[:ROWS].astype(BF)
        out[:, fold_cols(j)] = fold(matrix, value[ROWS:].astype(BF))
        cols = columns(j, BLK)
        copy = pltpu.make_async_copy(out.at[:, cols], out_ref.at[:, cols], osem.at[j])
        copy.start()
        outs.append(copy)

    for j in range(NG):
        copies[j].wait()
        emit(j, sel, grad[:, columns(j)])
    gates = gates_ref[...]
    gate = dot(gates, interleave(0))[0:1, :] + dot(gates, interleave(1))[1:2, :]
    gated = jnp.where(dot(rows, assignments(r0, r1)) == rank, gate, 0.0).astype(BF)
    hid_copy.wait()
    for j in range(NH):
        emit(NG + j, gated, hid[:, :, columns(j)].reshape(A, COL))
    for copy in outs:
        copy.wait()


def pack(ids, gates, grad, hid):
    return pl.pallas_call(
        pack_kernel,
        in_specs=[IN_VMEM, IN_VMEM, ANY, ANY],
        out_specs=ANY,
        out_shape=jax.ShapeDtypeStruct((ROWS, MSG), BF),
        scratch_shapes=[
            pltpu.VMEM((T, D), BF),
            pltpu.VMEM((T, 2, F), BF),
            pltpu.VMEM((ROWS, MSG), BF),
            pltpu.SemaphoreType.DMA((NG + 1,)),
            pltpu.SemaphoreType.DMA((NG + NH,)),
        ],
        compiler_params=PARAMS,
        name="pack",
    )(ids, gates, grad, hid)


def raw_kernel(dp_ref, msg_ref, own_ref, other_ref, out_ref, msg, w, acc, sem):
    own = pl.ds(pl.multiple_of(dp_ref[0] * COL, COL), COL)
    other = pl.ds(pl.multiple_of((1 - dp_ref[0]) * COL, COL), COL)
    copies = []
    for j in range(NG):
        block, cols = columns(j, BLK), columns(j)
        group = [
            pltpu.make_async_copy(msg_ref.at[:, block], msg.at[:, block], sem.at[j, 0]),
            pltpu.make_async_copy(own_ref.at[:, cols], w.at[own, cols], sem.at[j, 1]),
            pltpu.make_async_copy(other_ref.at[:, cols], w.at[other, cols], sem.at[j, 2]),
        ]
        for copy in group:
            copy.start()
        copies.append(group)
    matrix = unfold_matrix()
    for j in range(NG):
        for copy in copies[j]:
            copy.wait()
        over = unfold(matrix, msg[:, fold_cols(j)])
        rows = jnp.concatenate([msg[:, main_cols(j)], over], axis=0)
        value = dot_nt(rows, w[:, columns(j)])
        if j == 0:
            acc[...] = value
        else:
            acc[...] += value
    out_ref[:, :F] = acc[:ROWS, :].astype(BF)
    out_ref[:, F:] = fold(fold_matrix(), acc[ROWS:, :].astype(BF))


def raw_rows(dp, msg, own, other):
    return pl.pallas_call(
        raw_kernel,
        in_specs=[IN_SMEM, ANY, ANY, ANY],
        out_shape=jax.ShapeDtypeStruct((ROWS, RET), BF),
        scratch_shapes=[
            pltpu.VMEM((ROWS, NG * BLK), BF),
            pltpu.VMEM((F, D), BF),
            pltpu.VMEM((ROWS + OVER, F), F32),
            pltpu.SemaphoreType.DMA((NG, 3)),
        ],
        compiler_params=PARAMS,
        name="raw",
    )(dp, msg, own, other)


def grad_kernel(dp_ref, own_ref, got_ref, out_ref, msgs, hids, ht, out, sem, osem):
    sources = (own_ref, got_ref)
    half = pl.ds(pl.multiple_of((NG + dp_ref[0]) * BLK, FOLD), BLK)
    hid_copies = []
    for i, ref in enumerate(sources):
        copy = pltpu.make_async_copy(ref.at[:, half], hids.at[i], sem.at[NG, i])
        copy.start()
        hid_copies.append(copy)
    copies = []
    for j in range(NG):
        block = columns(j, BLK)
        group = []
        for i, ref in enumerate(sources):
            copy = pltpu.make_async_copy(ref.at[:, block], msgs.at[i, :, block], sem.at[j, i])
            copy.start()
            group.append(copy)
        copies.append(group)
    matrix = unfold_matrix()
    for i in range(2):
        hid_copies[i].wait()
        at = i * (ROWS + OVER)
        ht[:, at : at + ROWS] = hids[i, :, :COL].T
        ht[:, at + ROWS : at + ROWS + OVER] = unfold(matrix, hids[i, :, COL:]).T
    outs = []
    for j in range(NG):
        for copy in copies[j]:
            copy.wait()
        rows = []
        for i in range(2):
            rows.append(msgs[i, :, main_cols(j)])
            rows.append(unfold(matrix, msgs[i, :, fold_cols(j)]))
        cols = columns(j)
        out[:, cols] = dot(ht[...], jnp.concatenate(rows, axis=0)).astype(BF)
        copy = pltpu.make_async_copy(out.at[:, cols], out_ref.at[:, cols], osem.at[j])
        copy.start()
        outs.append(copy)
    for copy in outs:
        copy.wait()


def weight_rows(dp, own, got):
    return pl.pallas_call(
        grad_kernel,
        in_specs=[IN_SMEM, ANY, ANY],
        out_specs=ANY,
        out_shape=jax.ShapeDtypeStruct((COL, D), BF),
        scratch_shapes=[
            pltpu.VMEM((2, ROWS, NG * BLK), BF),
            pltpu.VMEM((2, ROWS, BLK), BF),
            pltpu.VMEM((COL, 2 * (ROWS + OVER)), BF),
            pltpu.VMEM((COL, D), BF),
            pltpu.SemaphoreType.DMA((NG + 1, 2)),
            pltpu.SemaphoreType.DMA((NG,)),
        ],
        compiler_params=PARAMS,
        name="weight_grad",
    )(dp, own, got)


def select_kernel(ids_ref, out_ref):
    r0, r1 = rank_maps(ids_ref[...])
    rows, rank = slots()
    chosen = (dot(rows, assignments(r0, r1)) == rank).astype(F32)
    out_ref[...] = chosen.T.astype(BF)


def select(ids):
    return pl.pallas_call(
        select_kernel,
        out_shape=jax.ShapeDtypeStruct((A, ROWS + OVER), BF),
        compiler_params=PARAMS,
        name="select",
    )(ids)


def combine_kernel(sel_ref, ret_ref, gates_ref, hid_ref, out_ref, gg_ref, part):
    over = unfold(unfold_matrix(), ret_ref[:, F:])
    raw = dot(sel_ref[...], jnp.concatenate([ret_ref[:, :F], over], axis=0))
    gates = gates_ref[...].astype(F32)
    row, token = iota((A, T), 0), iota((A, T), 1)
    spread = jnp.where(row == 2 * token, gates[0:1, :], 0.0)
    spread += jnp.where(row == 2 * token + 1, gates[1:2, :], 0.0)
    gate = jnp.sum(spread, axis=1, keepdims=True)
    out_ref[...] = (gate * raw).astype(BF).reshape(T, 2, F)
    product = hid_ref[...].reshape(A, F).astype(F32) * raw
    total = product[:, columns(0, 128)]
    for c in range(1, F // 128):
        total += product[:, columns(c, 128)]
    part[...] = total
    for k in range(2):
        rows = part[pl.ds(k, T, stride=2), :]
        gg_ref[k : k + 1, :] = jnp.sum(rows.T, axis=0, keepdims=True)


def combine(sel, ret, gates, hid):
    return pl.pallas_call(
        combine_kernel,
        out_shape=(jax.ShapeDtypeStruct((T, 2, F), BF), jax.ShapeDtypeStruct((2, T), F32)),
        scratch_shapes=[pltpu.VMEM((A, 128), F32)],
        compiler_params=PARAMS,
        name="combine",
    )(sel, ret, gates, hid)


def exchange(x):
    width = x.shape[1]
    swapped = lax.all_to_all(
        x.reshape(E, 8, width), "expert", split_axis=0, concat_axis=0, tiled=True
    )
    return swapped.reshape(ROWS, width)


def swap(x):
    return lax.ppermute(x, "dp", [(0, 1), (1, 0)])


def per_device(hidden, grad_out, gates, expert_ids, weight):
    dp = lax.axis_index("dp").astype(jnp.int32).reshape(1)
    ids = expert_ids.T
    own = weight[0]
    packed = pack(ids, gates.T, grad_out, hidden)
    other = swap(own)
    packed, other, dp = lax.optimization_barrier((packed, other, dp))
    msg = exchange(packed)
    raw = raw_rows(dp, msg, own, other)
    got = swap(msg)
    ids, msg, raw = lax.optimization_barrier((ids, msg, raw))
    ret = exchange(raw)
    sel = select(ids)
    weight_grad = weight_rows(dp, msg, got)
    ret, weight_grad = lax.optimization_barrier((ret, weight_grad))
    ret = pltpu.with_memory_space_constraint(ret, pltpu.VMEM)
    grad_hidden, grad_gates = combine(sel, ret, gates.T, hidden)
    return grad_hidden, grad_gates.T, weight_grad[None]


def solution(mesh):
    in_specs = (
        P(("dp", "expert"), None, None),
        P(("dp", "expert"), None),
        P(("dp", "expert"), None),
        P(("dp", "expert"), None),
        P("expert", "dp", None),
    )
    out_specs = (
        P(("dp", "expert"), None, None),
        P(("dp", "expert"), None),
        P("expert", "dp", None),
    )
    return jax.shard_map(
        per_device, mesh=mesh, in_specs=in_specs, out_specs=out_specs, check_vma=False
    )
```

time: 273 us -> 133 us (0.49)
  waiting for transfers between devices: 133 us -> 10.4 us
  blocking collectives: 0 us -> 83.1 us
  starting transfers between devices: 48.5 us -> 6 us
  Pallas kernels: 0 us -> 32.9 us
  matrix products: 29.9 us -> 0 us
  local copies, waits for them, and re-layouts: 27.7 us -> 0 us
  other arithmetic: 18.4 us -> 0 us
  between operations: 14.2 us -> 0.68 us
    all_to_all x5 -> x1, waiting for transfers between devices: 132 us -> 10.4 us  [exchange(): lax.all_to_all(x.reshape(E, 8, width), 'expert', split_axis=0, concat_axi...]
    all_to_all x0 -> x1, blocking collectives: none -> 83.1 us  [exchange(): lax.all_to_all(x.reshape(E, 8, width), 'expert', split_axis=0, concat_axi...]
    all_to_all x5 -> x1, starting transfers between devices: 48.5 us -> 5.91 us  [exchange(): lax.all_to_all(x.reshape(E, 8, width), 'expert', split_axis=0, concat_axi...]
    pallas_call x0 -> x5, Pallas kernels: none -> 32.9 us  [the longest x1 9.44 us: weight_rows(): pl.pallas_call(grad_kernel, in_specs=[IN_SMEM, ANY, ANY], out_specs=ANY,...]
    dot_general x5 -> x0, matrix products: 29.9 us -> none  [the longest x1 12.9 us: per_device(): lax.dot_general(hidden_rows, scaled, contract_rows, preferred_element_typ...]
    reshape x6 -> x0, local copies, waits for them, and re-layouts: 21.7 us -> none  [the longest x1 7.95 us: per_device(): grad_rows = received[1].reshape(slot_rows, width_d)]
    convert_element_type x4 -> x0, other arithmetic: 8.62 us -> none  [the longest x1 8.57 us: per_device(): (gate_rows.astype(jnp.float32)[:, None] * grad_rows.astype(jnp.float32))....]
    reduce_sum x4 -> x0, other arithmetic: 7.83 us -> none  [the longest x1 7.28 us: per_device(): jnp.sum(collected.astype(jnp.float32), axis=0).astype(jnp.bfloat16)[None]]
  transfers between devices with their start and end apart: 6 -> 3, of which waited for: 3 -> 1; matrix products, arithmetic and copies ran while one was open for 23% -> 0% of each run, Pallas kernels for 0% -> 22%
where the time goes in v2:
time: 133 us
  blocking collectives  83.1 us (62%)
  Pallas kernels  32.9 us (25%)
  waiting for transfers between devices  10.4 us (8%)
  starting transfers between devices  6 us (5%)
    all_to_all x1, blocking collectives, exchange(): lax.all_to_all(x.reshape(E, 8, width), 'expert', split_axis=0, concat_axi...  83.1 us
    all_to_all x1, waiting for transfers between devices, exchange(): lax.all_to_all(x.reshape(E, 8, width), 'expert', split_axis=0, concat_axi...  10.4 us
    pallas_call x1, Pallas kernels, weight_rows(): pl.pallas_call(grad_kernel, in_specs=[IN_SMEM, ANY, ANY], out_specs=ANY,...  9.44 us
    pallas_call x1, Pallas kernels, raw_rows(): pl.pallas_call(raw_kernel, in_specs=[IN_SMEM, ANY, ANY, ANY], out_shape=j...  8.95 us
    pallas_call x1, Pallas kernels, pack(): pl.pallas_call(pack_kernel, in_specs=[IN_VMEM, IN_VMEM, ANY, ANY], out_sp...  8.19 us
    all_to_all x1, starting transfers between devices, exchange(): lax.all_to_all(x.reshape(E, 8, width), 'expert', split_axis=0, concat_axi...  5.91 us
    pallas_call x1, Pallas kernels, combine(): pl.pallas_call(combine_kernel, out_shape=(jax.ShapeDtypeStruct((T, 2, F),...  4.09 us
  transfers between devices with their start and end apart: 3, of which 1 were waited for; matrix products, arithmetic and copies ran while one was open for 0% of the time, Pallas kernels for 22%

profile of v2, /device:TPU:0, one launch (start us, length us, event | category | flops | bytes accessed | tf_op | source)
XLA Modules:
  0.0 133.1 jit_solution(1847745865166517067)
XLA Ops:
  0.6 0.1 collective-permute-start
  0.7 8.2 %pack.1 = bf16[512,5760]{1,0:T(8,128)(2,1)} custom-call(s32[2,256]{1,0:T(2,128)} %bitcast.16, bf16[2,256]{1,0:T(2,128)(2,1)} %bitcast.18, bf16[256,3584]{1,0:T(8,128)(2,1)} %grad_ref.1, bf16[256,2,1024]{2,1,0:T(2,128)(2,1)} %hid_ref.3), custom_call_target="tpu_custom_call" | custom-call | tf_op jit(solution)/shard_map/pack/pallas_call | solution.py:153
  8.9 0.0 collective-permute-done.other_ref
  8.9 83.1 %all_to_all.10 = bf16[64,8,5760]{2,1,0:T(8,128)(2,1)} all-to-all(bf16[64,8,5760]{2,1,0:T(8,128)(2,1)} %bitcast.11), channel_id=1, replica_groups=mesh['dp'=2,'expert'=64] {'expert'}, dimensions={0} | all-to-all | bytes 11796480 | tf_op jit(solution)/shard_map/all_to_all | solution.py:321
  92.0 0.0 collective-permute-start.1
  92.0 9.0 %raw.1 = bf16[512,1280]{1,0:T(8,128)(2,1)} custom-call(s32[1]{0:T(128)} %bitcast.3.dp_ref, bf16[512,5760]{1,0:T(8,128)(2,1)} %bitcast.5.msg_ref.own_ref, bf16[512,3584]{1,0:T(8,128)(2,1)} %bitcast.14, bf16[512,3584]{1,0:T(8,128)(2,1)} %collective-permute-done.other_ref), custom_call_target="tpu_custom_call" | custom-call | tf_op jit(solution)/shard_map/raw/pallas_call | solution.py:200
  101.0 5.9 %all-to-all-start.1 = ((bf16[64,8,1280]{2,1,0:T(8,128)(2,1)}), bf16[64,8,1280]{2,1,0:T(8,128)(2,1)S(1)}, u32[]{:S(2)}, u32[]{:S(2)}) async-start(bf16[64,8,1280]{2,1,0:T(8,128)(2,1)} %bitcast.12), calls=%async_computation.1 | async-start | bytes 2621440 | tf_op jit(solution)/shard_map/all_to_all | solution.py:321
  106.9 2.3 %select.1.sel_ref = bf16[512,640]{1,0:T(8,128)(2,1)} custom-call(s32[2,256]{1,0:T(2,128)} %bitcast.17), custom_call_target="tpu_custom_call" | custom-call | tf_op jit(solution)/shard_map/select/pallas_call | solution.py:282
  109.2 0.0 collective-permute-done.1.got_ref
  109.2 9.4 %weight_grad.1 = bf16[512,3584]{1,0:T(8,128)(2,1)} custom-call(s32[1]{0:T(128)} %bitcast.3.dp_ref, bf16[512,5760]{1,0:T(8,128)(2,1)} %bitcast.5.msg_ref.own_ref, bf16[512,5760]{1,0:T(8,128)(2,1)} %collective-permute-done.1.got_ref), custom_call_target="tpu_custom_call" | custom-call | tf_op jit(solution)/shard_map/weight_grad/pallas_call | solution.py:256
  118.6 10.4 %all-to-all-done.1 = bf16[64,8,1280]{2,1,0:T(8,128)(2,1)S(1)} async-done(((bf16[64,8,1280]{2,1,0:T(8,128)(2,1)}), bf16[64,8,1280]{2,1,0:T(8,128)(2,1)S(1)}, u32[]{:S(2)}, u32[]{:S(2)}) %all-to-all-start.1) | async-done | bytes 1310752 | tf_op jit(solution)/shard_map/all_to_all | solution.py:321
  129.0 4.1 %combine.1 = (bf16[256,2,1024]{2,1,0:T(2,128)(2,1)}, f32[2,256]{1,0:T(2,128)}) custom-call(bf16[512,640]{1,0:T(8,128)(2,1)} %select.1.sel_ref, bf16[512,1280]{1,0:T(8,128)(2,1)S(1)} %bitcast.10, bf16[2,256]{1,0:T(2,128)(2,1)} %bitcast.19, bf16[256,2,1024]{2,1,0:T(2,128)(2,1)} %hid_ref.3), custom_call_target="tpu_custom_call" | custom-call | tf_op jit(solution)/shard_map/combine/pallas_call | solution.py:310
Async XLA Ops:
  0.6 8.3 %collective-permute-start = (bf16[512,3584]{1,0:T(8,128)(2,1)}, bf16[512,3584]{1,0:T(8,128)(2,1)}, u32[]{:S(2)}, u32[]{:S(2)}) collective-permute-start(bf16[512,3584]{1,0:T(8,128)(2,1)} %bitcast.13), channel_id=1, source_target_pairs={{0,64},{64,0},{1,65},{65,1},{2,66},{66,2},{3,67},{67,3},{4,68},{68... | collective-permute-start | bytes 11010056 | tf_op jit(solution)/shard_map/ppermute | solution.py:328
  92.0 17.2 %collective-permute-start.1 = (bf16[512,5760]{1,0:T(8,128)(2,1)}, bf16[512,5760]{1,0:T(8,128)(2,1)}, u32[]{:S(2)}, u32[]{:S(2)}) collective-permute-start(bf16[512,5760]{1,0:T(8,128)(2,1)} %bitcast.5.msg_ref.own_ref), channel_id=1, source_target_pairs={{0,64},{64,0},{1,65},{65,1},{2,66},{66,2},{3,67},{67,3},{4,68},{68... | collective-permute-start | bytes 17694728 | tf_op jit(solution)/shard_map/ppermute | solution.py:328
  101.0 28.1 %all-to-all-start.1 = ((bf16[64,8,1280]{2,1,0:T(8,128)(2,1)}), bf16[64,8,1280]{2,1,0:T(8,128)(2,1)S(1)}, u32[]{:S(2)}, u32[]{:S(2)}) async-start(bf16[64,8,1280]{2,1,0:T(8,128)(2,1)} %bitcast.12), calls=%async_computation.1 | async-start | bytes 2621440 | tf_op jit(solution)/shard_map/all_to_all | solution.py:321

commit v3 on v2

v3 whole, which is shorter than its diff:
```python
import jax
import jax.numpy as jnp
from jax import lax
from jax.experimental import pallas as pl
from jax.experimental.pallas import tpu as pltpu
from jax.sharding import PartitionSpec as P

T = 256
A = 512
E = 64
D = 3584
F = 1024
COL = 512
FOLD = COL // 4
BLK = COL + FOLD
NG = D // COL
NH = F // COL
MSG = BLK * (NG + NH)
RET = F + F // 4
ROWS = 512
OVER = 128
BF = jnp.bfloat16
F32 = jnp.float32
PARAMS = pltpu.CompilerParams(vmem_limit_bytes=36 * 1024 * 1024)
IN_HBM = pl.BlockSpec(memory_space=pltpu.HBM)
IN_VMEM = pl.BlockSpec(memory_space=pltpu.VMEM)
IN_SMEM = pl.BlockSpec(memory_space=pltpu.SMEM)


def keep(x):
    return pltpu.with_memory_space_constraint(x, pltpu.VMEM)


def iota(shape, axis):
    return lax.broadcasted_iota(jnp.int32, shape, axis)


def dot(a, b):
    return jnp.dot(a, b, preferred_element_type=F32)


def dot_nt(a, b):
    return lax.dot_general(a, b, (((1,), (1,)), ((), ())), preferred_element_type=F32)


def columns(j, width=COL):
    return slice(j * width, (j + 1) * width)


def main_cols(j):
    return slice(j * BLK, j * BLK + COL)


def fold_cols(j):
    return slice(j * BLK + COL, (j + 1) * BLK)


def trade(x):
    row = iota((1, 8, 128), 1)
    low, even = row < 4, (row & 2) == 0

    def mix(p, q, shift, first):
        return (
            jnp.where(first, p, pltpu.roll(q, shift, 1)),
            jnp.where(first, pltpu.roll(p, 8 - shift, 1), q),
        )

    b0, b2 = mix(x[0], x[2], 4, low)
    b1, b3 = mix(x[1], x[3], 4, low)
    return mix(b0, b1, 2, even) + mix(b2, b3, 2, even)


def fold(over):
    width = over.shape[1] // 4
    out = []
    for c in range(width // 128):
        parts = []
        for q in range(4):
            at = q * width + c * 128
            parts.append(over[:, at : at + 128].reshape(16, 8, 128))
        out.append(jnp.stack(trade(parts), axis=1).reshape(ROWS, 128).astype(BF))
    return jnp.concatenate(out, axis=1)


def unfold(folded):
    quarters = [[], [], [], []]
    for c in range(folded.shape[1] // 128):
        part = folded[:, columns(c, 128)].astype(F32).reshape(16, 4, 8, 128)
        for q, rows in enumerate(trade([part[:, i] for i in range(4)])):
            quarters[q].append(rows.reshape(OVER, 128).astype(BF))
    return jnp.concatenate([rows for quarter in quarters for rows in quarter], axis=1)


def rank_maps(ids):
    experts = iota((E, T), 0)
    o0 = (ids[0:1, :] == experts).astype(F32)
    o1 = (ids[1:2, :] == experts).astype(F32)
    earlier = (iota((T, T), 0) < iota((T, T), 1)).astype(F32).astype(BF)
    count = dot((o0 + o1).astype(BF), earlier)
    return o0 * (count + 1.0), o1 * (count + 1.0)


def slots():
    i = iota((ROWS + OVER, 1), 0)
    main = i < ROWS
    expert = jnp.where(main, jnp.right_shift(i, 3), jnp.right_shift(i - ROWS, 1))
    rank = jnp.where(main, (i & 7) + 1, (i & 1) + 9)
    rows = (expert == iota((ROWS + OVER, E), 1)).astype(F32).astype(BF)
    return rows, rank.astype(F32)


def interleave(k):
    return (iota((T, A), 1) == 2 * iota((T, A), 0) + k).astype(F32).astype(BF)


def assignments(r0, r1):
    by_assign = dot(r0.astype(BF), interleave(0)) + dot(r1.astype(BF), interleave(1))
    return by_assign.astype(BF)


def pack_kernel(ids_hbm, gates_hbm, grad_hbm, hid_hbm, out_ref, ids, gates, grad, hid, sem):
    first = slice(0, 3 * COL)
    rest = slice(3 * COL, D)
    copies = [
        pltpu.make_async_copy(ids_hbm, ids, sem.at[0]),
        pltpu.make_async_copy(gates_hbm, gates, sem.at[1]),
        pltpu.make_async_copy(grad_hbm.at[:, first], grad.at[:, first], sem.at[2]),
        pltpu.make_async_copy(grad_hbm.at[:, rest], grad.at[:, rest], sem.at[3]),
        pltpu.make_async_copy(hid_hbm, hid, sem.at[4]),
    ]
    for copy in copies:
        copy.start()
    rows, rank = slots()
    copies[0].wait()
    copies[1].wait()
    r0, r1 = rank_maps(ids[...])
    sel = (dot(rows, (r0 + r1).astype(BF)) == rank).astype(F32).astype(BF)
    gate = dot(gates[...], interleave(0))[0:1, :] + dot(gates[...], interleave(1))[1:2, :]
    gated = jnp.where(dot(rows, assignments(r0, r1)) == rank, gate, 0.0).astype(BF)

    def emit(j, chosen, x):
        value = dot(chosen, x)
        out_ref[:, main_cols(j)] = value[:ROWS].astype(BF)
        out_ref[:, fold_cols(j)] = fold(value[ROWS:])

    copies[2].wait()
    for j in range(3):
        emit(j, sel, grad[:, columns(j)])
    copies[3].wait()
    for j in range(3, NG):
        emit(j, sel, grad[:, columns(j)])
    copies[4].wait()
    for j in range(NH):
        emit(NG + j, gated, hid[:, :, columns(j)].reshape(A, COL))


def pack(ids, gates, grad, hid):
    return pl.pallas_call(
        pack_kernel,
        in_specs=[IN_HBM, IN_HBM, IN_HBM, IN_HBM],
        out_specs=IN_VMEM,
        out_shape=pltpu.VMEM((ROWS, MSG), BF),
        scratch_shapes=[
            pltpu.VMEM((2, T), jnp.int32),
            pltpu.VMEM((2, T), BF),
            pltpu.VMEM((T, D), BF),
            pltpu.VMEM((T, 2, F), BF),
            pltpu.SemaphoreType.DMA((5,)),
        ],
        compiler_params=pltpu.CompilerParams(vmem_limit_bytes=50 * 1024 * 1024),
        name="pack",
    )(ids, gates, grad, hid)


def raw_kernel(
    dp_ref, msg_ref, own_ref, other_hbm, out_hbm, keep_hbm, other, over, acc, out, last, sem
):
    weight_copy = pltpu.make_async_copy(other_hbm, other, sem.at[4])
    weight_copy.start()
    outs = [pltpu.make_async_copy(msg_ref, keep_hbm, sem.at[3])]
    outs[0].start()
    for i, weight in enumerate((own_ref, other)):
        value = None
        if i == 1:
            weight_copy.wait()
        for j in range(NG):
            if i == 0:
                over[:, columns(j)] = unfold(msg_ref[:, fold_cols(j)])
            rows = jnp.concatenate([msg_ref[:, main_cols(j)], over[:, columns(j)]], axis=0)
            part = dot_nt(rows, weight[:, columns(j)])
            value = part if value is None else value + part
        half = dp_ref[0] if i == 0 else 1 - dp_ref[0]
        cols = pl.ds(pl.multiple_of(half * COL, COL), COL)
        out[i] = value[:ROWS].astype(BF)
        acc[:, cols] = value[ROWS:]
        copy = pltpu.make_async_copy(out.at[i], out_hbm.at[:, cols], sem.at[i])
        copy.start()
        outs.append(copy)
    last[...] = fold(acc[...])
    copy = pltpu.make_async_copy(last, out_hbm.at[:, F:], sem.at[2])
    copy.start()
    for copy in outs + [copy]:
        copy.wait()


def raw_rows(dp, msg, own, other):
    return pl.pallas_call(
        raw_kernel,
        in_specs=[IN_SMEM, IN_VMEM, IN_VMEM, IN_HBM],
        out_specs=(IN_HBM, IN_HBM),
        out_shape=(
            jax.ShapeDtypeStruct((ROWS, RET), BF),
            jax.ShapeDtypeStruct((ROWS, MSG), BF),
        ),
        scratch_shapes=[
            pltpu.VMEM((COL, D), BF),
            pltpu.VMEM((OVER, D), BF),
            pltpu.VMEM((OVER, F), F32),
            pltpu.VMEM((2, ROWS, COL), BF),
            pltpu.VMEM((ROWS, F // 4), BF),
            pltpu.SemaphoreType.DMA((5,)),
        ],
        compiler_params=pltpu.CompilerParams(vmem_limit_bytes=32 * 1024 * 1024),
        name="raw",
    )(dp, keep(msg), keep(own), other)


def grad_kernel(dp_ref, own_ref, got_ref, out_ref, msgs, hids, ht, out, sem, osem):
    sources = (own_ref, got_ref)
    half = pl.ds(pl.multiple_of((NG + dp_ref[0]) * BLK, FOLD), BLK)
    hid_copies = []
    for i, ref in enumerate(sources):
        copy = pltpu.make_async_copy(ref.at[:, half], hids.at[i], sem.at[NG, i])
        copy.start()
        hid_copies.append(copy)
    copies = []
    for j in range(NG):
        block = columns(j, BLK)
        group = []
        for i, ref in enumerate(sources):
            copy = pltpu.make_async_copy(ref.at[:, block], msgs.at[i, :, block], sem.at[j, i])
            copy.start()
            group.append(copy)
        copies.append(group)
    for i in range(2):
        hid_copies[i].wait()
        at = i * (ROWS + OVER)
        ht[:, at : at + ROWS] = hids[i, :, :COL].T
        ht[:, at + ROWS : at + ROWS + OVER] = unfold(hids[i, :, COL:]).T
    outs = []
    for j in range(NG):
        for copy in copies[j]:
            copy.wait()
        rows = []
        for i in range(2):
            rows.append(msgs[i, :, main_cols(j)])
            rows.append(unfold(msgs[i, :, fold_cols(j)]))
        cols = columns(j)
        out[:, cols] = dot(ht[...], jnp.concatenate(rows, axis=0)).astype(BF)
        copy = pltpu.make_async_copy(out.at[:, cols], out_ref.at[:, cols], osem.at[j])
        copy.start()
        outs.append(copy)
    for copy in outs:
        copy.wait()


def weight_rows(dp, own, got):
    return pl.pallas_call(
        grad_kernel,
        in_specs=[IN_SMEM, IN_HBM, IN_HBM],
        out_specs=IN_HBM,
        out_shape=jax.ShapeDtypeStruct((COL, D), BF),
        scratch_shapes=[
            pltpu.VMEM((2, ROWS, NG * BLK), BF),
            pltpu.VMEM((2, ROWS, BLK), BF),
            pltpu.VMEM((COL, 2 * (ROWS + OVER)), BF),
            pltpu.VMEM((COL, D), BF),
            pltpu.SemaphoreType.DMA((NG + 1, 2)),
            pltpu.SemaphoreType.DMA((NG,)),
        ],
        compiler_params=PARAMS,
        name="weight_grad",
    )(dp, own, got)


def select_kernel(ids_ref, out_ref):
    r0, r1 = rank_maps(ids_ref[...])
    rows, rank = slots()
    chosen = (dot(rows, assignments(r0, r1)) == rank).astype(F32)
    out_ref[...] = chosen.T.astype(BF)


def select(ids):
    return pl.pallas_call(
        select_kernel,
        out_shape=jax.ShapeDtypeStruct((A, ROWS + OVER), BF),
        compiler_params=PARAMS,
        name="select",
    )(ids)


def combine_kernel(sel_ref, ret_ref, gates_ref, hid_ref, out_ref, gg_ref, part):
    over = unfold(ret_ref[:, F:])
    raw = dot(sel_ref[...], jnp.concatenate([ret_ref[:, :F], over], axis=0))
    gates = gates_ref[...].astype(F32)
    row, token = iota((A, T), 0), iota((A, T), 1)
    spread = jnp.where(row == 2 * token, gates[0:1, :], 0.0)
    spread += jnp.where(row == 2 * token + 1, gates[1:2, :], 0.0)
    gate = jnp.sum(spread, axis=1, keepdims=True)
    out_ref[...] = (gate * raw).astype(BF).reshape(T, 2, F)
    product = hid_ref[...].reshape(A, F).astype(F32) * raw
    total = product[:, columns(0, 128)]
    for c in range(1, F // 128):
        total += product[:, columns(c, 128)]
    part[...] = total
    for k in range(2):
        rows = part[pl.ds(k, T, stride=2), :]
        gg_ref[k : k + 1, :] = jnp.sum(rows.T, axis=0, keepdims=True)


def combine(sel, ret, gates, hid):
    return pl.pallas_call(
        combine_kernel,
        out_shape=(jax.ShapeDtypeStruct((T, 2, F), BF), jax.ShapeDtypeStruct((2, T), F32)),
        scratch_shapes=[pltpu.VMEM((A, 128), F32)],
        compiler_params=PARAMS,
        name="combine",
    )(sel, ret, gates, hid)


def exchange(x):
    width = x.shape[1]
    swapped = lax.all_to_all(
        x.reshape(E, 8, width), "expert", split_axis=0, concat_axis=0, tiled=True
    )
    return swapped.reshape(ROWS, width)


def swap(x):
    return lax.ppermute(x, "dp", [(0, 1), (1, 0)])


def per_device(hidden, grad_out, gates, expert_ids, weight):
    dp = lax.axis_index("dp").astype(jnp.int32).reshape(1)
    ids = expert_ids.T
    own = weight[0]
    packed = pack(ids, gates.T, grad_out, hidden)
    other = swap(own)
    packed, other, dp = lax.optimization_barrier((packed, other, dp))
    msg = exchange(packed)
    raw, msg = raw_rows(dp, msg, own, other)
    got = swap(msg)
    ids, raw = lax.optimization_barrier((ids, raw))
    ret = exchange(raw)
    sel = select(ids)
    weight_grad = weight_rows(dp, msg, got)
    ret, weight_grad = lax.optimization_barrier((ret, weight_grad))
    ret = keep(ret)
    grad_hidden, grad_gates = combine(sel, ret, gates.T, hidden)
    return grad_hidden, grad_gates.T, weight_grad[None]


def solution(mesh):
    in_specs = (
        P(("dp", "expert"), None, None),
        P(("dp", "expert"), None),
        P(("dp", "expert"), None),
        P(("dp", "expert"), None),
        P("expert", "dp", None),
    )
    out_specs = (
        P(("dp", "expert"), None, None),
        P(("dp", "expert"), None),
        P("expert", "dp", None),
    )
    return jax.shard_map(
        per_device, mesh=mesh, in_specs=in_specs, out_specs=out_specs, check_vma=False
    )
```

time: 133 us -> 129 us (0.970)
  Pallas kernels: 32.9 us -> 24.1 us
  waiting for transfers between devices: 10.4 us -> 15.4 us
    pallas_call x3, Pallas kernels: 26.6 us -> 20.6 us  [the longest x1 8.61 us: weight_rows(): pl.pallas_call(grad_kernel, in_specs=[IN_SMEM, IN_HBM, IN_HBM], out_specs...]
    ppermute x2, waiting for transfers between devices: 0.01 us -> 5.77 us  [swap(): return lax.ppermute(x, 'dp', [(0, 1), (1, 0)])]
    pallas_call x1, Pallas kernels: 2.27 us -> 0.74 us  [select(): pl.pallas_call(select_kernel, out_shape=jax.ShapeDtypeStruct((A, ROWS + O...]
  transfers between devices with their start and end apart: 3 -> 3, of which waited for: 1 -> 3; matrix products, arithmetic and copies ran while one was open for 0% -> 0% of each run, Pallas kernels for 22% -> 10%
where the time goes in v3:
time: 129 us
  blocking collectives  82.7 us (64%)
  Pallas kernels  24.1 us (19%)
  waiting for transfers between devices  15.4 us (12%)
  starting transfers between devices  6.18 us (5%)
    all_to_all x1, blocking collectives, exchange(): lax.all_to_all(x.reshape(E, 8, width), 'expert', split_axis=0, concat_axi...  82.7 us
    all_to_all x1, waiting for transfers between devices, exchange(): lax.all_to_all(x.reshape(E, 8, width), 'expert', split_axis=0, concat_axi...  9.6 us
    pallas_call x1, Pallas kernels, weight_rows(): pl.pallas_call(grad_kernel, in_specs=[IN_SMEM, IN_HBM, IN_HBM], out_specs...  8.61 us
    pallas_call x1, Pallas kernels, raw_rows(): pl.pallas_call(raw_kernel, in_specs=[IN_SMEM, IN_VMEM, IN_VMEM, IN_HBM],...  7.87 us
    all_to_all x1, starting transfers between devices, exchange(): lax.all_to_all(x.reshape(E, 8, width), 'expert', split_axis=0, concat_axi...  6 us
    ppermute x2, waiting for transfers between devices, swap(): return lax.ppermute(x, 'dp', [(0, 1), (1, 0)])  5.77 us
    pallas_call x1, Pallas kernels, pack(): pl.pallas_call(pack_kernel, in_specs=[IN_HBM, IN_HBM, IN_HBM, IN_HBM], ou...  4.08 us
    pallas_call x1, Pallas kernels, combine(): pl.pallas_call(combine_kernel, out_shape=(jax.ShapeDtypeStruct((T, 2, F),...  2.82 us
  transfers between devices with their start and end apart: 3, of which 3 were waited for; matrix products, arithmetic and copies ran while one was open for 0% of the time, Pallas kernels for 10%

profile of v3, /device:TPU:0, one launch (start us, length us, event | category | flops | bytes accessed | tf_op | source)
XLA Modules:
  0.0 129.1 jit_solution(15160594149618456761)
XLA Ops:
  0.6 0.1 collective-permute-start
  0.7 4.1 %pack.1 = bf16[512,5760]{1,0:T(8,128)(2,1)S(1)} custom-call(s32[2,256]{1,0:T(2,128)} %bitcast.15, bf16[2,256]{1,0:T(2,128)(2,1)} %bitcast.17, bf16[256,3584]{1,0:T(8,128)(2,1)} %grad_hbm.1, bf16[256,2,1024]{2,1,0:T(2,128)(2,1)} %hid_ref.1), custom_call_target="tpu_custom_call" | custom-call | tf_op jit(solution)/shard_map/pack/pallas_call | solution.py:158
  4.8 2.6 %collective-permute-done.other_hbm = bf16[512,3584]{1,0:T(8,128)(2,1)} collective-permute-done((bf16[512,3584]{1,0:T(8,128)(2,1)}, bf16[512,3584]{1,0:T(8,128)(2,1)}, u32[]{:S(2)}, u32[]{:S(2)}) %collective-permute-start) | collective-permute-done | bytes 3670048 | tf_op jit(solution)/shard_map/ppermute | solution.py:340
  7.5 0.0 copy-start.1
  7.5 82.7 %all_to_all.10 = bf16[64,8,5760]{2,1,0:T(8,128)(2,1)S(1)} all-to-all(bf16[64,8,5760]{2,1,0:T(8,128)(2,1)S(1)} %bitcast.11), channel_id=1, replica_groups=mesh['dp'=2,'expert'=64] {'expert'}, dimensions={0} | all-to-all | bytes 11796480 | tf_op jit(solution)/shard_map/all_to_all | solution.py:333
  90.1 0.0 copy-done.1
  90.1 0.0 copy-start.2
  90.1 7.9 %raw.1 = (bf16[512,1280]{1,0:T(8,128)(2,1)}, bf16[512,5760]{1,0:T(8,128)(2,1)}) custom-call(s32[1]{0:T(128)} %bitcast.3.dp_ref, bf16[512,5760]{1,0:T(8,128)(2,1)S(1)} %bitcast.10, bf16[512,3584]{1,0:T(8,128)(2,1)S(1)} %bitcast.14, bf16[512,3584]{1,0:T(8,128)(2,1)} %collective-permute-done.other_hbm), custom_call_target="tpu_custom_call" | custom-call | tf_op jit(solution)/shard_map/raw/pallas_call | solution.py:207
  98.0 0.1 collective-permute-start.1
  98.1 6.0 %all-to-all-start.1 = ((bf16[64,8,1280]{2,1,0:T(8,128)(2,1)}), bf16[64,8,1280]{2,1,0:T(8,128)(2,1)S(1)}, u32[]{:S(2)}, u32[]{:S(2)}) async-start(bf16[64,8,1280]{2,1,0:T(8,128)(2,1)} %bitcast.6), calls=%async_computation.1 | async-start | bytes 2621440 | tf_op jit(solution)/shard_map/all_to_all | solution.py:333
  104.1 0.0 copy-done.2
  104.1 0.7 select.1.sel_ref
  104.9 0.0 copy-start
  104.9 0.0 copy-start.3
  104.9 3.1 %collective-permute-done.1.got_ref = bf16[512,5760]{1,0:T(8,128)(2,1)} collective-permute-done((bf16[512,5760]{1,0:T(8,128)(2,1)}, bf16[512,5760]{1,0:T(8,128)(2,1)}, u32[]{:S(2)}, u32[]{:S(2)}) %collective-permute-start.1) | collective-permute-done | bytes 5898272 | tf_op jit(solution)/shard_map/ppermute | solution.py:340
  108.0 8.6 %weight_grad.1 = bf16[512,3584]{1,0:T(8,128)(2,1)} custom-call(s32[1]{0:T(128)} %bitcast.3.dp_ref, bf16[512,5760]{1,0:T(8,128)(2,1)} %get-tuple-element.20.own_ref, bf16[512,5760]{1,0:T(8,128)(2,1)} %collective-permute-done.1.got_ref), custom_call_target="tpu_custom_call" | custom-call | tf_op jit(solution)/shard_map/weight_grad/pallas_call | solution.py:268
  116.7 9.6 %all-to-all-done.1 = bf16[64,8,1280]{2,1,0:T(8,128)(2,1)S(1)} async-done(((bf16[64,8,1280]{2,1,0:T(8,128)(2,1)}), bf16[64,8,1280]{2,1,0:T(8,128)(2,1)S(1)}, u32[]{:S(2)}, u32[]{:S(2)}) %all-to-all-start.1) | async-done | bytes 1310752 | tf_op jit(solution)/shard_map/all_to_all | solution.py:333
  126.3 0.0 copy-done
  126.3 0.0 copy-done.3
  126.3 2.8 %combine.1 = (bf16[256,2,1024]{2,1,0:T(2,128)(2,1)}, f32[2,256]{1,0:T(2,128)}) custom-call(bf16[512,640]{1,0:T(8,128)(2,1)S(1)} %select.1.sel_ref, bf16[512,1280]{1,0:T(8,128)(2,1)S(1)} %bitcast.12, bf16[2,256]{1,0:T(2,128)(2,1)S(1)} %bitcast.18, bf16[256,2,1024]{2,1,0:T(2,128)(2,1)S(1)} %copy-done), custom_call_target="tpu_custom_call" | custom-call | tf_op jit(solution)/shard_map/combine/pallas_call | solution.py:322
Async XLA Ops:
  0.6 6.8 %collective-permute-start = (bf16[512,3584]{1,0:T(8,128)(2,1)}, bf16[512,3584]{1,0:T(8,128)(2,1)}, u32[]{:S(2)}, u32[]{:S(2)}) collective-permute-start(bf16[512,3584]{1,0:T(8,128)(2,1)} %bitcast.13), channel_id=1, source_target_pairs={{0,64},{64,0},{1,65},{65,1},{2,66},{66,2},{3,67},{67,3},{4,68},{68... | collective-permute-start | bytes 11010056 | tf_op jit(solution)/shard_map/ppermute | solution.py:340
  7.5 82.7 %copy-start.1 = (bf16[1,512,3584]{2,1,0:T(8,128)(2,1)S(1)}, bf16[1,512,3584]{2,1,0:T(8,128)(2,1)}, u32[]{:S(2)}) copy-start(bf16[1,512,3584]{2,1,0:T(8,128)(2,1)} %param.9) | copy-start | bytes 11010052
  90.1 14.0 %copy-start.2 = (s32[256,2]{0,1:T(2,128)S(1)}, s32[256,2]{0,1:T(2,128)}, u32[]{:S(2)}) copy-start(s32[256,2]{0,1:T(2,128)} %param.8) | copy-start | bytes 6148
  98.0 10.0 %collective-permute-start.1 = (bf16[512,5760]{1,0:T(8,128)(2,1)}, bf16[512,5760]{1,0:T(8,128)(2,1)}, u32[]{:S(2)}, u32[]{:S(2)}) collective-permute-start(bf16[512,5760]{1,0:T(8,128)(2,1)} %get-tuple-element.20.own_ref), channel_id=1, source_target_pairs={{0,64},{64,0},{1,65},{65,1},{2,66},{66,2},{3,67},{67,3},{4,68},{68... | collective-permute-start | bytes 17694728 | tf_op jit(solution)/shard_map/ppermute | solution.py:340
  98.1 28.1 %all-to-all-start.1 = ((bf16[64,8,1280]{2,1,0:T(8,128)(2,1)}), bf16[64,8,1280]{2,1,0:T(8,128)(2,1)S(1)}, u32[]{:S(2)}, u32[]{:S(2)}) async-start(bf16[64,8,1280]{2,1,0:T(8,128)(2,1)} %bitcast.6), calls=%async_computation.1 | async-start | bytes 2621440 | tf_op jit(solution)/shard_map/all_to_all | solution.py:333
  104.9 21.4 %copy-start = (bf16[256,2,1024]{2,1,0:T(2,128)(2,1)S(1)}, bf16[256,2,1024]{2,1,0:T(2,128)(2,1)}, u32[]{:S(2)}) copy-start(bf16[256,2,1024]{2,1,0:T(2,128)(2,1)} %hid_ref.1) | copy-start | bytes 3145732
  104.9 21.4 %copy-start.3 = (bf16[256,2]{0,1:T(2,128)(2,1)S(1)}, bf16[256,2]{0,1:T(2,128)(2,1)}, u32[]{:S(2)}) copy-start(bf16[256,2]{0,1:T(2,128)(2,1)} %param.7) | copy-start | bytes 3076

commit v4 on v3

--- a/solution.py
+++ b/solution.py
@@ -71,14 +71,15 @@
 
 
 def fold(over):
+    groups = over.shape[0] // 8
     width = over.shape[1] // 4
     out = []
     for c in range(width // 128):
         parts = []
         for q in range(4):
             at = q * width + c * 128
-            parts.append(over[:, at : at + 128].reshape(16, 8, 128))
-        out.append(jnp.stack(trade(parts), axis=1).reshape(ROWS, 128).astype(BF))
+            parts.append(over[:, at : at + 128].reshape(groups, 8, 128))
+        out.append(jnp.stack(trade(parts), axis=1).reshape(groups * 32, 128).astype(BF))
     return jnp.concatenate(out, axis=1)
 
 
@@ -177,29 +178,43 @@
 ):
     weight_copy = pltpu.make_async_copy(other_hbm, other, sem.at[4])
     weight_copy.start()
-    outs = [pltpu.make_async_copy(msg_ref, keep_hbm, sem.at[3])]
-    outs[0].start()
-    for i, weight in enumerate((own_ref, other)):
+    copies = [pltpu.make_async_copy(msg_ref, keep_hbm, sem.at[3])]
+    copies[0].start()
+
+    def multiply(weight, main, extra):
         value = None
-        if i == 1:
-            weight_copy.wait()
         for j in range(NG):
-            if i == 0:
-                over[:, columns(j)] = unfold(msg_ref[:, fold_cols(j)])
-            rows = jnp.concatenate([msg_ref[:, main_cols(j)], over[:, columns(j)]], axis=0)
+            first = j * BLK
+            rows = jnp.concatenate(
+                [msg_ref[main, first : first + COL], over[extra, columns(j)]], axis=0
+            )
             part = dot_nt(rows, weight[:, columns(j)])
             value = part if value is None else value + part
-        half = dp_ref[0] if i == 0 else 1 - dp_ref[0]
-        cols = pl.ds(pl.multiple_of(half * COL, COL), COL)
-        out[i] = value[:ROWS].astype(BF)
-        acc[:, cols] = value[ROWS:]
-        copy = pltpu.make_async_copy(out.at[i], out_hbm.at[:, cols], sem.at[i])
+        return value
+
+    def send(source, target, i):
+        copy = pltpu.make_async_copy(source, target, sem.at[i])
         copy.start()
-        outs.append(copy)
-    last[...] = fold(acc[...])
-    copy = pltpu.make_async_copy(last, out_hbm.at[:, F:], sem.at[2])
-    copy.start()
-    for copy in outs + [copy]:
+        copies.append(copy)
+
+    for j in range(NG):
+        over[:, columns(j)] = unfold(msg_ref[:, fold_cols(j)])
+    cols = pl.ds(pl.multiple_of(dp_ref[0] * COL, COL), COL)
+    value = multiply(own_ref, slice(0, ROWS), slice(0, OVER))
+    out[0] = value[:ROWS].astype(BF)
+    acc[:, cols] = value[ROWS:]
+    send(out.at[0], out_hbm.at[:, cols], 0)
+    weight_copy.wait()
+    cols = pl.ds(pl.multiple_of((1 - dp_ref[0]) * COL, COL), COL)
+    for b in range(2):
+        main, extra = columns(b, ROWS // 2), columns(b, OVER // 2)
+        value = multiply(other, main, extra)
+        out[1, main] = value[: ROWS // 2].astype(BF)
+        acc[extra, cols] = value[ROWS // 2 :]
+        send(out.at[1, main], out_hbm.at[main, cols], 1 + 4 * b)
+        last[main] = fold(acc[extra, :])
+        send(last.at[main], out_hbm.at[main, F:], 2 + 4 * b)
+    for copy in copies:
         copy.wait()
 
 
@@ -218,9 +233,9 @@
             pltpu.VMEM((OVER, F), F32),
             pltpu.VMEM((2, ROWS, COL), BF),
             pltpu.VMEM((ROWS, F // 4), BF),
-            pltpu.SemaphoreType.DMA((5,)),
+            pltpu.SemaphoreType.DMA((7,)),
         ],
-        compiler_params=pltpu.CompilerParams(vmem_limit_bytes=32 * 1024 * 1024),
+        compiler_params=pltpu.CompilerParams(vmem_limit_bytes=44 * 1024 * 1024),
         name="raw",
     )(dp, keep(msg), keep(own), other)
 
@@ -278,54 +293,68 @@
             pltpu.SemaphoreType.DMA((NG + 1, 2)),
             pltpu.SemaphoreType.DMA((NG,)),
         ],
-        compiler_params=PARAMS,
+        compiler_params=pltpu.CompilerParams(vmem_limit_bytes=44 * 1024 * 1024),
         name="weight_grad",
     )(dp, own, got)
 
 
-def select_kernel(ids_ref, out_ref):
+def prepare_kernel(ids_ref, gates_ref, hid_ref, sel_ref, rows_ref, gate_ref):
     r0, r1 = rank_maps(ids_ref[...])
     rows, rank = slots()
     chosen = (dot(rows, assignments(r0, r1)) == rank).astype(F32)
-    out_ref[...] = chosen.T.astype(BF)
-
-
-def select(ids):
-    return pl.pallas_call(
-        select_kernel,
-        out_shape=jax.ShapeDtypeStruct((A, ROWS + OVER), BF),
-        compiler_params=PARAMS,
-        name="select",
-    )(ids)
-
-
-def combine_kernel(sel_ref, ret_ref, gates_ref, hid_ref, out_ref, gg_ref, part):
-    over = unfold(ret_ref[:, F:])
-    raw = dot(sel_ref[...], jnp.concatenate([ret_ref[:, :F], over], axis=0))
+    sel_ref[...] = chosen.T.astype(BF)
+    rows_ref[...] = hid_ref[...].reshape(A, F)
     gates = gates_ref[...].astype(F32)
     row, token = iota((A, T), 0), iota((A, T), 1)
     spread = jnp.where(row == 2 * token, gates[0:1, :], 0.0)
     spread += jnp.where(row == 2 * token + 1, gates[1:2, :], 0.0)
     gate = jnp.sum(spread, axis=1, keepdims=True)
-    out_ref[...] = (gate * raw).astype(BF).reshape(T, 2, F)
-    product = hid_ref[...].reshape(A, F).astype(F32) * raw
-    total = product[:, columns(0, 128)]
-    for c in range(1, F // 128):
-        total += product[:, columns(c, 128)]
+    gate_ref[...] = jnp.broadcast_to(gate, (A, 128))
+
+
+def prepare(ids, gates, hid):
+    return pl.pallas_call(
+        prepare_kernel,
+        in_specs=[IN_VMEM, IN_VMEM, IN_VMEM],
+        out_specs=(IN_VMEM, IN_VMEM, IN_VMEM),
+        out_shape=(
+            pltpu.VMEM((A, ROWS + OVER), BF),
+            pltpu.VMEM((A, F), BF),
+            pltpu.VMEM((A, 128), F32),
+        ),
+        compiler_params=PARAMS,
+        name="prepare",
+    )(ids, gates, hid)
+
+
+def combine_kernel(sel_ref, ret_ref, gate_ref, hid_ref, out_ref, gg_ref, part):
+    over = unfold(ret_ref[:, F:])
+    gate = jnp.concatenate([gate_ref[...]] * (COL // 128), axis=1)
+    total = None
+    for j in range(NH):
+        cols = columns(j)
+        raw = dot(sel_ref[...], jnp.concatenate([ret_ref[:, cols], over[:, cols]], axis=0))
+        out_ref[:, :, cols] = (gate * raw).astype(BF).reshape(T, 2, COL)
+        product = hid_ref[:, cols].astype(F32) * raw
+        for c in range(COL // 128):
+            piece = product[:, columns(c, 128)]
+            total = piece if total is None else total + piece
     part[...] = total
     for k in range(2):
         rows = part[pl.ds(k, T, stride=2), :]
         gg_ref[k : k + 1, :] = jnp.sum(rows.T, axis=0, keepdims=True)
 
 
-def combine(sel, ret, gates, hid):
+def combine(sel, ret, gate, hid):
     return pl.pallas_call(
         combine_kernel,
+        in_specs=[IN_VMEM, IN_VMEM, IN_VMEM, IN_VMEM],
+        out_specs=(IN_VMEM, IN_VMEM),
         out_shape=(jax.ShapeDtypeStruct((T, 2, F), BF), jax.ShapeDtypeStruct((2, T), F32)),
         scratch_shapes=[pltpu.VMEM((A, 128), F32)],
         compiler_params=PARAMS,
         name="combine",
-    )(sel, ret, gates, hid)
+    )(keep(sel), keep(ret), keep(gate), keep(hid))
 
 
 def exchange(x):
@@ -352,11 +381,10 @@
     got = swap(msg)
     ids, raw = lax.optimization_barrier((ids, raw))
     ret = exchange(raw)
-    sel = select(ids)
+    sel, hid_rows, gate = prepare(ids, gates.T, hidden)
     weight_grad = weight_rows(dp, msg, got)
     ret, weight_grad = lax.optimization_barrier((ret, weight_grad))
-    ret = keep(ret)
-    grad_hidden, grad_gates = combine(sel, ret, gates.T, hidden)
+    grad_hidden, grad_gates = combine(sel, ret, gate, hid_rows)
     return grad_hidden, grad_gates.T, weight_grad[None]
 
 

time: 129 us -> 129 us (level)
  local copies, waits for them, and re-layouts: 0.02 us -> 4.23 us
  waiting for transfers between devices: 15.4 us -> 11.3 us
    unnamed x8 -> x18, local copies, waits for them, and re-layouts: 0.02 us -> 4.23 us
    all_to_all x1, waiting for transfers between devices: 9.6 us -> 7.16 us  [exchange(): lax.all_to_all(x.reshape(E, 8, width), 'expert', split_axis=0, concat_axi...]
    ppermute x2, waiting for transfers between devices: 5.77 us -> 4.11 us  [swap(): return lax.ppermute(x, 'dp', [(0, 1), (1, 0)])]
where the time goes in v4:
time: 129 us; the launch traced here: 128 us
  blocking collectives  82.7 us (64%)
  Pallas kernels  23.2 us (18%)
  waiting for transfers between devices  11.3 us (9%)
  starting transfers between devices  6.18 us (5%)
  local copies, waits for them, and re-layouts  4.23 us (3%)
    all_to_all x1, blocking collectives, exchange(): lax.all_to_all(x.reshape(E, 8, width), 'expert', split_axis=0, concat_axi...  82.7 us
    pallas_call x1, Pallas kernels, weight_rows(): pl.pallas_call(grad_kernel, in_specs=[IN_SMEM, IN_HBM, IN_HBM], out_specs...  8.36 us
    pallas_call x1, Pallas kernels, raw_rows(): pl.pallas_call(raw_kernel, in_specs=[IN_SMEM, IN_VMEM, IN_VMEM, IN_HBM],...  7.81 us
    all_to_all x1, waiting for transfers between devices, exchange(): lax.all_to_all(x.reshape(E, 8, width), 'expert', split_axis=0, concat_axi...  7.16 us
    all_to_all x1, starting transfers between devices, exchange(): lax.all_to_all(x.reshape(E, 8, width), 'expert', split_axis=0, concat_axi...  6 us
    unnamed x18, local copies, waits for them, and re-layouts  4.23 us
    ppermute x2, waiting for transfers between devices, swap(): return lax.ppermute(x, 'dp', [(0, 1), (1, 0)])  4.11 us
    pallas_call x1, Pallas kernels, pack(): pl.pallas_call(pack_kernel, in_specs=[IN_HBM, IN_HBM, IN_HBM, IN_HBM], ou...  4.08 us
  transfers between devices with their start and end apart: 3, of which 3 were waited for; matrix products, arithmetic and copies ran while one was open for 0% of the time, Pallas kernels for 10%

profile of v4, /device:TPU:0, one launch (start us, length us, event | category | flops | bytes accessed | tf_op | source)
XLA Modules:
  0.0 128.3 jit_solution(15595685485393446062)
XLA Ops:
  0.6 0.1 collective-permute-start
  0.7 4.1 %pack.1 = bf16[512,5760]{1,0:T(8,128)(2,1)S(1)} custom-call(s32[2,256]{1,0:T(2,128)} %bitcast.15, bf16[2,256]{1,0:T(2,128)(2,1)} %bitcast.17, bf16[256,3584]{1,0:T(8,128)(2,1)} %grad_hbm.1, bf16[256,2,1024]{2,1,0:T(2,128)(2,1)} %hid_ref.1), custom_call_target="tpu_custom_call" | custom-call | tf_op jit(solution)/shard_map/pack/pallas_call | solution.py:159
  4.8 2.6 %collective-permute-done.other_hbm = bf16[512,3584]{1,0:T(8,128)(2,1)} collective-permute-done((bf16[512,3584]{1,0:T(8,128)(2,1)}, bf16[512,3584]{1,0:T(8,128)(2,1)}, u32[]{:S(2)}, u32[]{:S(2)}) %collective-permute-start) | collective-permute-done | bytes 3670048 | tf_op jit(solution)/shard_map/ppermute | solution.py:369
  7.5 0.0 copy-start.2
  7.5 82.7 %all_to_all.10 = bf16[64,8,5760]{2,1,0:T(8,128)(2,1)S(1)} all-to-all(bf16[64,8,5760]{2,1,0:T(8,128)(2,1)S(1)} %bitcast.11), channel_id=1, replica_groups=mesh['dp'=2,'expert'=64] {'expert'}, dimensions={0} | all-to-all | bytes 11796480 | tf_op jit(solution)/shard_map/all_to_all | solution.py:362
  90.1 0.0 copy-done.2
  90.1 0.0 copy-start.1
  90.1 0.0 copy-start.7
  90.1 0.0 copy-start.8
  90.2 7.8 %raw.1 = (bf16[512,1280]{1,0:T(8,128)(2,1)}, bf16[512,5760]{1,0:T(8,128)(2,1)}) custom-call(s32[1]{0:T(128)} %bitcast.3.dp_ref, bf16[512,5760]{1,0:T(8,128)(2,1)S(1)} %bitcast.10, bf16[512,3584]{1,0:T(8,128)(2,1)S(1)} %bitcast.14, bf16[512,3584]{1,0:T(8,128)(2,1)} %collective-permute-done.other_hbm), custom_call_target="tpu_custom_call" | custom-call | tf_op jit(solution)/shard_map/raw/pallas_call | solution.py:222
  98.0 0.1 collective-permute-start.1
  98.1 6.0 %all-to-all-start.1 = ((bf16[64,8,1280]{2,1,0:T(8,128)(2,1)}), bf16[64,8,1280]{2,1,0:T(8,128)(2,1)S(1)}, u32[]{:S(2)}, u32[]{:S(2)}) async-start(bf16[64,8,1280]{2,1,0:T(8,128)(2,1)} %bitcast.20), calls=%async_computation.1 | async-start | bytes 2621440 | tf_op jit(solution)/shard_map/all_to_all | solution.py:362
  104.1 0.0 copy-done.1
  104.1 0.0 copy-done.7
  104.1 0.0 copy-done.8
  104.1 0.9 prepare.1
  105.0 0.0 copy-start.3
  105.0 0.8 copy-done.3
  105.8 0.0 copy-start.5
  105.8 0.7 copy-done.5
  106.5 1.5 %collective-permute-done.1.got_ref = bf16[512,5760]{1,0:T(8,128)(2,1)} collective-permute-done((bf16[512,5760]{1,0:T(8,128)(2,1)}, bf16[512,5760]{1,0:T(8,128)(2,1)}, u32[]{:S(2)}, u32[]{:S(2)}) %collective-permute-start.1) | collective-permute-done | bytes 5898272 | tf_op jit(solution)/shard_map/ppermute | solution.py:369
  108.0 0.0 copy-start
  108.0 2.7 %copy-done = bf16[512,5760]{1,0:T(8,128)(2,1)S(1)} copy-done((bf16[512,5760]{1,0:T(8,128)(2,1)S(1)}, bf16[512,5760]{1,0:T(8,128)(2,1)}, u32[]{:S(2)}) %copy-start) | copy-done | bytes 5898264
  110.7 0.0 copy-start.4
  110.7 0.0 copy-start.6
  110.7 8.4 %weight_grad.1 = bf16[512,3584]{1,0:T(8,128)(2,1)} custom-call(s32[1]{0:T(128)} %bitcast.3.dp_ref, bf16[512,5760]{1,0:T(8,128)(2,1)S(1)} %copy-done, bf16[512,5760]{1,0:T(8,128)(2,1)} %collective-permute-done.1.got_ref), custom_call_target="tpu_custom_call" | custom-call | tf_op jit(solution)/shard_map/weight_grad/pallas_call | solution.py:283
  119.0 7.2 %all-to-all-done.1 = bf16[64,8,1280]{2,1,0:T(8,128)(2,1)S(1)} async-done(((bf16[64,8,1280]{2,1,0:T(8,128)(2,1)}), bf16[64,8,1280]{2,1,0:T(8,128)(2,1)S(1)}, u32[]{:S(2)}, u32[]{:S(2)}) %all-to-all-start.1) | async-done | bytes 1310752 | tf_op jit(solution)/shard_map/all_to_all | solution.py:362
  126.2 0.0 copy-done.4
  126.2 0.0 copy-done.6
  126.2 2.1 %combine.1 = (bf16[256,2,1024]{2,1,0:T(2,128)(2,1)}, f32[2,256]{1,0:T(2,128)}) custom-call(bf16[512,640]{1,0:T(8,128)(2,1)S(1)} %copy-done.4, bf16[512,1280]{1,0:T(8,128)(2,1)S(1)} %bitcast.12, f32[512,128]{1,0:T(8,128)S(1)} %copy-done.6, bf16[512,1024]{1,0:T(8,128)(2,1)S(1)} %get-tuple-element.27.hid_ref), custom_call_target="tpu_custom_call" | custom-call | tf_op jit(solution)/shard_map/combine/pallas_call | solution.py:349
Async XLA Ops:
  0.6 6.8 %collective-permute-start = (bf16[512,3584]{1,0:T(8,128)(2,1)}, bf16[512,3584]{1,0:T(8,128)(2,1)}, u32[]{:S(2)}, u32[]{:S(2)}) collective-permute-start(bf16[512,3584]{1,0:T(8,128)(2,1)} %bitcast.13), channel_id=1, source_target_pairs={{0,64},{64,0},{1,65},{65,1},{2,66},{66,2},{3,67},{67,3},{4,68},{68... | collective-permute-start | bytes 11010056 | tf_op jit(solution)/shard_map/ppermute | solution.py:369
  7.5 82.7 %copy-start.2 = (bf16[1,512,3584]{2,1,0:T(8,128)(2,1)S(1)}, bf16[1,512,3584]{2,1,0:T(8,128)(2,1)}, u32[]{:S(2)}) copy-start(bf16[1,512,3584]{2,1,0:T(8,128)(2,1)} %param.9) | copy-start | bytes 11010052
  90.1 13.9 %copy-start.1 = (bf16[256,2,1024]{2,1,0:T(2,128)(2,1)S(1)}, bf16[256,2,1024]{2,1,0:T(2,128)(2,1)}, u32[]{:S(2)}) copy-start(bf16[256,2,1024]{2,1,0:T(2,128)(2,1)} %hid_ref.1) | copy-start | bytes 3145732
  90.1 13.9 %copy-start.7 = (s32[256,2]{0,1:T(2,128)S(1)}, s32[256,2]{0,1:T(2,128)}, u32[]{:S(2)}) copy-start(s32[256,2]{0,1:T(2,128)} %param.8) | copy-start | bytes 6148
  90.1 13.9 %copy-start.8 = (bf16[256,2]{0,1:T(2,128)(2,1)S(1)}, bf16[256,2]{0,1:T(2,128)(2,1)}, u32[]{:S(2)}) copy-start(bf16[256,2]{0,1:T(2,128)(2,1)} %param.7) | copy-start | bytes 3076
  98.0 10.0 %collective-permute-start.1 = (bf16[512,5760]{1,0:T(8,128)(2,1)}, bf16[512,5760]{1,0:T(8,128)(2,1)}, u32[]{:S(2)}, u32[]{:S(2)}) collective-permute-start(bf16[512,5760]{1,0:T(8,128)(2,1)} %get-tuple-element.24.own_ref), channel_id=1, source_target_pairs={{0,64},{64,0},{1,65},{65,1},{2,66},{66,2},{3,67},{67,3},{4,68},{68... | collective-permute-start | bytes 17694728 | tf_op jit(solution)/shard_map/ppermute | solution.py:369
  98.1 28.1 %all-to-all-start.1 = ((bf16[64,8,1280]{2,1,0:T(8,128)(2,1)}), bf16[64,8,1280]{2,1,0:T(8,128)(2,1)S(1)}, u32[]{:S(2)}, u32[]{:S(2)}) async-start(bf16[64,8,1280]{2,1,0:T(8,128)(2,1)} %bitcast.20), calls=%async_computation.1 | async-start | bytes 2621440 | tf_op jit(solution)/shard_map/all_to_all | solution.py:362
  105.0 0.8 copy-start.3
  105.8 0.7 copy-start.5
  108.0 2.7 %copy-start = (bf16[512,5760]{1,0:T(8,128)(2,1)S(1)}, bf16[512,5760]{1,0:T(8,128)(2,1)}, u32[]{:S(2)}) copy-start(bf16[512,5760]{1,0:T(8,128)(2,1)} %get-tuple-element.24.own_ref) | copy-start | bytes 17694724
  110.7 15.5 %copy-start.4 = (bf16[512,640]{1,0:T(8,128)(2,1)S(1)}, bf16[512,640]{1,0:T(8,128)(2,1)}, u32[]{:S(2)}) copy-start(bf16[512,640]{1,0:T(8,128)(2,1)} %copy-done.3) | copy-start | bytes 1966084
  110.7 15.5 %copy-start.6 = (f32[512,128]{1,0:T(8,128)S(1)}, f32[512,128]{1,0:T(8,128)}, u32[]{:S(2)}) copy-start(f32[512,128]{1,0:T(8,128)} %copy-done.5) | copy-start | bytes 786436

commit v5 on v4

--- a/solution.py
+++ b/solution.py
@@ -178,12 +178,13 @@
 ):
     weight_copy = pltpu.make_async_copy(other_hbm, other, sem.at[4])
     weight_copy.start()
-    copies = [pltpu.make_async_copy(msg_ref, keep_hbm, sem.at[3])]
-    copies[0].start()
+    copies = []
 
     def multiply(weight, main, extra):
         value = None
         for j in range(NG):
+            if weight is own_ref:
+                over[:, columns(j)] = unfold(msg_ref[:, fold_cols(j)])
             first = j * BLK
             rows = jnp.concatenate(
                 [msg_ref[main, first : first + COL], over[extra, columns(j)]], axis=0
@@ -197,13 +198,12 @@
         copy.start()
         copies.append(copy)
 
-    for j in range(NG):
-        over[:, columns(j)] = unfold(msg_ref[:, fold_cols(j)])
     cols = pl.ds(pl.multiple_of(dp_ref[0] * COL, COL), COL)
     value = multiply(own_ref, slice(0, ROWS), slice(0, OVER))
     out[0] = value[:ROWS].astype(BF)
     acc[:, cols] = value[ROWS:]
     send(out.at[0], out_hbm.at[:, cols], 0)
+    send(msg_ref, keep_hbm, 3)
     weight_copy.wait()
     cols = pl.ds(pl.multiple_of((1 - dp_ref[0]) * COL, COL), COL)
     for b in range(2):

time: 129 us -> 127 us (0.984)
  Pallas kernels: 23.2 us -> 21.4 us
    pallas_call x1, Pallas kernels: 7.81 us -> 5.98 us  [raw_rows(): pl.pallas_call(raw_kernel, in_specs=[IN_SMEM, IN_VMEM, IN_VMEM, IN_HBM],...]
  transfers between devices with their start and end apart: 3 -> 3, of which waited for: 3 -> 3; matrix products, arithmetic and copies ran while one was open for 0% -> 0% of each run, Pallas kernels for 10% -> 11%
where the time goes in v5:
time: 127 us
  blocking collectives  82.7 us (65%)
  Pallas kernels  21.4 us (17%)
  waiting for transfers between devices  11.3 us (9%)
  starting transfers between devices  6.18 us (5%)
  local copies, waits for them, and re-layouts  4.23 us (3%)
    all_to_all x1, blocking collectives, exchange(): lax.all_to_all(x.reshape(E, 8, width), 'expert', split_axis=0, concat_axi...  82.7 us
    pallas_call x1, Pallas kernels, weight_rows(): pl.pallas_call(grad_kernel, in_specs=[IN_SMEM, IN_HBM, IN_HBM], out_specs...  8.36 us
    all_to_all x1, waiting for transfers between devices, exchange(): lax.all_to_all(x.reshape(E, 8, width), 'expert', split_axis=0, concat_axi...  7.17 us
    all_to_all x1, starting transfers between devices, exchange(): lax.all_to_all(x.reshape(E, 8, width), 'expert', split_axis=0, concat_axi...  6.01 us
    pallas_call x1, Pallas kernels, raw_rows(): pl.pallas_call(raw_kernel, in_specs=[IN_SMEM, IN_VMEM, IN_VMEM, IN_HBM],...  5.98 us
    unnamed x18, local copies, waits for them, and re-layouts  4.23 us
    ppermute x2, waiting for transfers between devices, swap(): return lax.ppermute(x, 'dp', [(0, 1), (1, 0)])  4.11 us
    pallas_call x1, Pallas kernels, pack(): pl.pallas_call(pack_kernel, in_specs=[IN_HBM, IN_HBM, IN_HBM, IN_HBM], ou...  4.08 us
  transfers between devices with their start and end apart: 3, of which 3 were waited for; matrix products, arithmetic and copies ran while one was open for 0% of the time, Pallas kernels for 11%

profile of v5, /device:TPU:0, one launch (start us, length us, event | category | flops | bytes accessed | tf_op | source)
XLA Modules:
  0.0 126.5 jit_solution(8269836812672167433)
XLA Ops:
  0.6 0.1 collective-permute-start
  0.7 4.1 %pack.1 = bf16[512,5760]{1,0:T(8,128)(2,1)S(1)} custom-call(s32[2,256]{1,0:T(2,128)} %bitcast.15, bf16[2,256]{1,0:T(2,128)(2,1)} %bitcast.17, bf16[256,3584]{1,0:T(8,128)(2,1)} %grad_hbm.1, bf16[256,2,1024]{2,1,0:T(2,128)(2,1)} %hid_ref.1), custom_call_target="tpu_custom_call" | custom-call | tf_op jit(solution)/shard_map/pack/pallas_call | solution.py:159
  4.8 2.6 %collective-permute-done.other_hbm = bf16[512,3584]{1,0:T(8,128)(2,1)} collective-permute-done((bf16[512,3584]{1,0:T(8,128)(2,1)}, bf16[512,3584]{1,0:T(8,128)(2,1)}, u32[]{:S(2)}, u32[]{:S(2)}) %collective-permute-start) | collective-permute-done | bytes 3670048 | tf_op jit(solution)/shard_map/ppermute | solution.py:369
  7.5 0.0 copy-start.2
  7.5 82.7 %all_to_all.10 = bf16[64,8,5760]{2,1,0:T(8,128)(2,1)S(1)} all-to-all(bf16[64,8,5760]{2,1,0:T(8,128)(2,1)S(1)} %bitcast.11), channel_id=1, replica_groups=mesh['dp'=2,'expert'=64] {'expert'}, dimensions={0} | all-to-all | bytes 11796480 | tf_op jit(solution)/shard_map/all_to_all | solution.py:362
  90.1 0.0 copy-done.2
  90.1 0.0 copy-start.1
  90.1 0.0 copy-start.7
  90.1 0.0 copy-start.8
  90.2 6.0 %raw.1 = (bf16[512,1280]{1,0:T(8,128)(2,1)}, bf16[512,5760]{1,0:T(8,128)(2,1)}) custom-call(s32[1]{0:T(128)} %bitcast.3.dp_ref, bf16[512,5760]{1,0:T(8,128)(2,1)S(1)} %bitcast.10, bf16[512,3584]{1,0:T(8,128)(2,1)S(1)} %bitcast.14, bf16[512,3584]{1,0:T(8,128)(2,1)} %collective-permute-done.other_hbm), custom_call_target="tpu_custom_call" | custom-call | tf_op jit(solution)/shard_map/raw/pallas_call | solution.py:222
  96.1 0.1 collective-permute-start.1
  96.2 6.0 %all-to-all-start.1 = ((bf16[64,8,1280]{2,1,0:T(8,128)(2,1)}), bf16[64,8,1280]{2,1,0:T(8,128)(2,1)S(1)}, u32[]{:S(2)}, u32[]{:S(2)}) async-start(bf16[64,8,1280]{2,1,0:T(8,128)(2,1)} %bitcast.20), calls=%async_computation.1 | async-start | bytes 2621440 | tf_op jit(solution)/shard_map/all_to_all | solution.py:362
  102.2 0.0 copy-done.1
  102.3 0.0 copy-done.7
  102.3 0.0 copy-done.8
  102.3 0.9 prepare.1
  103.1 0.0 copy-start.3
  103.2 0.8 copy-done.3
  104.0 0.0 copy-start.5
  104.0 0.7 copy-done.5
  104.7 1.5 %collective-permute-done.1.got_ref = bf16[512,5760]{1,0:T(8,128)(2,1)} collective-permute-done((bf16[512,5760]{1,0:T(8,128)(2,1)}, bf16[512,5760]{1,0:T(8,128)(2,1)}, u32[]{:S(2)}, u32[]{:S(2)}) %collective-permute-start.1) | collective-permute-done | bytes 5898272 | tf_op jit(solution)/shard_map/ppermute | solution.py:369
  106.2 0.0 copy-start
  106.2 2.7 %copy-done = bf16[512,5760]{1,0:T(8,128)(2,1)S(1)} copy-done((bf16[512,5760]{1,0:T(8,128)(2,1)S(1)}, bf16[512,5760]{1,0:T(8,128)(2,1)}, u32[]{:S(2)}) %copy-start) | copy-done | bytes 5898264
  108.8 0.0 copy-start.4
  108.8 0.0 copy-start.6
  108.8 8.4 %weight_grad.1 = bf16[512,3584]{1,0:T(8,128)(2,1)} custom-call(s32[1]{0:T(128)} %bitcast.3.dp_ref, bf16[512,5760]{1,0:T(8,128)(2,1)S(1)} %copy-done, bf16[512,5760]{1,0:T(8,128)(2,1)} %collective-permute-done.1.got_ref), custom_call_target="tpu_custom_call" | custom-call | tf_op jit(solution)/shard_map/weight_grad/pallas_call | solution.py:283
  117.2 7.2 %all-to-all-done.1 = bf16[64,8,1280]{2,1,0:T(8,128)(2,1)S(1)} async-done(((bf16[64,8,1280]{2,1,0:T(8,128)(2,1)}), bf16[64,8,1280]{2,1,0:T(8,128)(2,1)S(1)}, u32[]{:S(2)}, u32[]{:S(2)}) %all-to-all-start.1) | async-done | bytes 1310752 | tf_op jit(solution)/shard_map/all_to_all | solution.py:362
  124.4 0.0 copy-done.4
  124.4 0.0 copy-done.6
  124.4 2.1 %combine.1 = (bf16[256,2,1024]{2,1,0:T(2,128)(2,1)}, f32[2,256]{1,0:T(2,128)}) custom-call(bf16[512,640]{1,0:T(8,128)(2,1)S(1)} %copy-done.4, bf16[512,1280]{1,0:T(8,128)(2,1)S(1)} %bitcast.12, f32[512,128]{1,0:T(8,128)S(1)} %copy-done.6, bf16[512,1024]{1,0:T(8,128)(2,1)S(1)} %get-tuple-element.27.hid_ref), custom_call_target="tpu_custom_call" | custom-call | tf_op jit(solution)/shard_map/combine/pallas_call | solution.py:349
Async XLA Ops:
  0.6 6.8 %collective-permute-start = (bf16[512,3584]{1,0:T(8,128)(2,1)}, bf16[512,3584]{1,0:T(8,128)(2,1)}, u32[]{:S(2)}, u32[]{:S(2)}) collective-permute-start(bf16[512,3584]{1,0:T(8,128)(2,1)} %bitcast.13), channel_id=1, source_target_pairs={{0,64},{64,0},{1,65},{65,1},{2,66},{66,2},{3,67},{67,3},{4,68},{68... | collective-permute-start | bytes 11010056 | tf_op jit(solution)/shard_map/ppermute | solution.py:369
  7.5 82.7 %copy-start.2 = (bf16[1,512,3584]{2,1,0:T(8,128)(2,1)S(1)}, bf16[1,512,3584]{2,1,0:T(8,128)(2,1)}, u32[]{:S(2)}) copy-start(bf16[1,512,3584]{2,1,0:T(8,128)(2,1)} %param.9) | copy-start | bytes 11010052
  90.1 12.1 %copy-start.1 = (bf16[256,2,1024]{2,1,0:T(2,128)(2,1)S(1)}, bf16[256,2,1024]{2,1,0:T(2,128)(2,1)}, u32[]{:S(2)}) copy-start(bf16[256,2,1024]{2,1,0:T(2,128)(2,1)} %hid_ref.1) | copy-start | bytes 3145732
  90.1 12.1 %copy-start.7 = (s32[256,2]{0,1:T(2,128)S(1)}, s32[256,2]{0,1:T(2,128)}, u32[]{:S(2)}) copy-start(s32[256,2]{0,1:T(2,128)} %param.8) | copy-start | bytes 6148
  90.1 12.1 %copy-start.8 = (bf16[256,2]{0,1:T(2,128)(2,1)S(1)}, bf16[256,2]{0,1:T(2,128)(2,1)}, u32[]{:S(2)}) copy-start(bf16[256,2]{0,1:T(2,128)(2,1)} %param.7) | copy-start | bytes 3076
  96.1 10.0 %collective-permute-start.1 = (bf16[512,5760]{1,0:T(8,128)(2,1)}, bf16[512,5760]{1,0:T(8,128)(2,1)}, u32[]{:S(2)}, u32[]{:S(2)}) collective-permute-start(bf16[512,5760]{1,0:T(8,128)(2,1)} %get-tuple-element.24.own_ref), channel_id=1, source_target_pairs={{0,64},{64,0},{1,65},{65,1},{2,66},{66,2},{3,67},{67,3},{4,68},{68... | collective-permute-start | bytes 17694728 | tf_op jit(solution)/shard_map/ppermute | solution.py:369
  96.2 28.1 %all-to-all-start.1 = ((bf16[64,8,1280]{2,1,0:T(8,128)(2,1)}), bf16[64,8,1280]{2,1,0:T(8,128)(2,1)S(1)}, u32[]{:S(2)}, u32[]{:S(2)}) async-start(bf16[64,8,1280]{2,1,0:T(8,128)(2,1)} %bitcast.20), calls=%async_computation.1 | async-start | bytes 2621440 | tf_op jit(solution)/shard_map/all_to_all | solution.py:362
  103.1 0.8 copy-start.3
  104.0 0.7 copy-start.5
  106.2 2.7 %copy-start = (bf16[512,5760]{1,0:T(8,128)(2,1)S(1)}, bf16[512,5760]{1,0:T(8,128)(2,1)}, u32[]{:S(2)}) copy-start(bf16[512,5760]{1,0:T(8,128)(2,1)} %get-tuple-element.24.own_ref) | copy-start | bytes 17694724
  108.8 15.5 %copy-start.4 = (bf16[512,640]{1,0:T(8,128)(2,1)S(1)}, bf16[512,640]{1,0:T(8,128)(2,1)}, u32[]{:S(2)}) copy-start(bf16[512,640]{1,0:T(8,128)(2,1)} %copy-done.3) | copy-start | bytes 1966084
  108.8 15.5 %copy-start.6 = (f32[512,128]{1,0:T(8,128)S(1)}, f32[512,128]{1,0:T(8,128)}, u32[]{:S(2)}) copy-start(f32[512,128]{1,0:T(8,128)} %copy-done.5) | copy-start | bytes 786436

commit v6 on v5

--- a/solution.py
+++ b/solution.py
@@ -105,6 +105,7 @@
     i = iota((ROWS + OVER, 1), 0)
     main = i < ROWS
     expert = jnp.where(main, jnp.right_shift(i, 3), jnp.right_shift(i - ROWS, 1))
+    expert = (expert * 21) & (E - 1)
     rank = jnp.where(main, (i & 7) + 1, (i & 1) + 9)
     rows = (expert == iota((ROWS + OVER, E), 1)).astype(F32).astype(BF)
     return rows, rank.astype(F32)
@@ -360,7 +361,12 @@
 def exchange(x):
     width = x.shape[1]
     swapped = lax.all_to_all(
-        x.reshape(E, 8, width), "expert", split_axis=0, concat_axis=0, tiled=True
+        x.reshape(E, 8, width),
+        "expert",
+        split_axis=0,
+        concat_axis=0,
+        axis_index_groups=[[i * 21 % E for i in range(E)]],
+        tiled=True,
     )
     return swapped.reshape(ROWS, width)
 

time: 127 us -> 124 us (0.976)
  blocking collectives: 82.7 us -> 80.3 us
  waiting for transfers between devices: 11.3 us -> 8.97 us
  starting transfers between devices: 6.18 us -> 7.55 us
    all_to_all x1, blocking collectives: 82.7 us -> 80.3 us  [exchange(): lax.all_to_all(x.reshape(E, 8, width), 'expert', split_axis=0, concat_axi...]
    ppermute x2, waiting for transfers between devices: 4.11 us -> 2.73 us  [swap(): return lax.ppermute(x, 'dp', [(0, 1), (1, 0)])]
    all_to_all x1, starting transfers between devices: 6.01 us -> 7.38 us  [exchange(): lax.all_to_all(x.reshape(E, 8, width), 'expert', split_axis=0, concat_axi...]
where the time goes in v6:
time: 124 us; the launch traced here: 123 us
  blocking collectives  80.3 us (65%)
  Pallas kernels  21.4 us (17%)
  waiting for transfers between devices  8.97 us (7%)
  starting transfers between devices  7.55 us (6%)
  local copies, waits for them, and re-layouts  4.23 us (3%)
    all_to_all x1, blocking collectives, exchange(): lax.all_to_all(x.reshape(E, 8, width), 'expert', split_axis=0, concat_axi...  80.3 us
    pallas_call x1, Pallas kernels, weight_rows(): pl.pallas_call(grad_kernel, in_specs=[IN_SMEM, IN_HBM, IN_HBM], out_specs...  8.36 us
    all_to_all x1, starting transfers between devices, exchange(): lax.all_to_all(x.reshape(E, 8, width), 'expert', split_axis=0, concat_axi...  7.38 us
    all_to_all x1, waiting for transfers between devices, exchange(): lax.all_to_all(x.reshape(E, 8, width), 'expert', split_axis=0, concat_axi...  6.24 us
    pallas_call x1, Pallas kernels, raw_rows(): pl.pallas_call(raw_kernel, in_specs=[IN_SMEM, IN_VMEM, IN_VMEM, IN_HBM],...  5.98 us
    unnamed x18, local copies, waits for them, and re-layouts  4.23 us
    pallas_call x1, Pallas kernels, pack(): pl.pallas_call(pack_kernel, in_specs=[IN_HBM, IN_HBM, IN_HBM, IN_HBM], ou...  4.08 us
    ppermute x2, waiting for transfers between devices, swap(): return lax.ppermute(x, 'dp', [(0, 1), (1, 0)])  2.73 us
  transfers between devices with their start and end apart: 3, of which 3 were waited for; matrix products, arithmetic and copies ran while one was open for 0% of the time, Pallas kernels for 11%

profile of v6, /device:TPU:0, one launch (start us, length us, event | category | flops | bytes accessed | tf_op | source)
XLA Modules:
  0.0 123.2 jit_solution(11474958519944958648)
XLA Ops:
  0.6 0.1 collective-permute-start
  0.7 4.1 %pack.1 = bf16[512,5760]{1,0:T(8,128)(2,1)S(1)} custom-call(s32[2,256]{1,0:T(2,128)} %bitcast.15, bf16[2,256]{1,0:T(2,128)(2,1)} %bitcast.17, bf16[256,3584]{1,0:T(8,128)(2,1)} %grad_hbm.1, bf16[256,2,1024]{2,1,0:T(2,128)(2,1)} %hid_ref.1), custom_call_target="tpu_custom_call" | custom-call | tf_op jit(solution)/shard_map/pack/pallas_call | solution.py:160
  4.8 2.6 %collective-permute-done.other_hbm = bf16[512,3584]{1,0:T(8,128)(2,1)} collective-permute-done((bf16[512,3584]{1,0:T(8,128)(2,1)}, bf16[512,3584]{1,0:T(8,128)(2,1)}, u32[]{:S(2)}, u32[]{:S(2)}) %collective-permute-start) | collective-permute-done | bytes 3670048 | tf_op jit(solution)/shard_map/ppermute | solution.py:375
  7.5 0.0 copy-start.2
  7.5 80.3 %all_to_all.10 = bf16[64,8,5760]{2,1,0:T(8,128)(2,1)S(1)} all-to-all(bf16[64,8,5760]{2,1,0:T(8,128)(2,1)S(1)} %bitcast.11), channel_id=1, replica_groups={{0,21,42,63,20,41,62,19,40,61,18,39,60,17,38,59,16,37,58,15,36,57,14,35..., dimensions={0} | all-to-all | bytes 11796480 | tf_op jit(solution)/shard_map/all_to_all | solution.py:363
  87.8 0.0 copy-done.2
  87.8 0.0 copy-start.1
  87.8 0.0 copy-start.7
  87.8 0.0 copy-start.8
  87.8 6.0 %raw.1 = (bf16[512,1280]{1,0:T(8,128)(2,1)}, bf16[512,5760]{1,0:T(8,128)(2,1)}) custom-call(s32[1]{0:T(128)} %bitcast.3.dp_ref, bf16[512,5760]{1,0:T(8,128)(2,1)S(1)} %bitcast.10, bf16[512,3584]{1,0:T(8,128)(2,1)S(1)} %bitcast.14, bf16[512,3584]{1,0:T(8,128)(2,1)} %collective-permute-done.other_hbm), custom_call_target="tpu_custom_call" | custom-call | tf_op jit(solution)/shard_map/raw/pallas_call | solution.py:223
  93.8 0.1 collective-permute-start.1
  93.9 7.4 %all-to-all-start.1 = ((bf16[64,8,1280]{2,1,0:T(8,128)(2,1)}), bf16[64,8,1280]{2,1,0:T(8,128)(2,1)S(1)}, u32[]{:S(2)}, u32[]{:S(2)}) async-start(bf16[64,8,1280]{2,1,0:T(8,128)(2,1)} %bitcast.20), calls=%async_computation.1 | async-start | bytes 2621440 | tf_op jit(solution)/shard_map/all_to_all | solution.py:363
  101.3 0.0 copy-done.1
  101.3 0.0 copy-done.7
  101.3 0.0 copy-done.8
  101.3 0.9 prepare.1
  102.2 0.0 copy-start.3
  102.2 0.8 copy-done.3
  103.0 0.0 copy-start.5
  103.0 0.7 copy-done.5
  103.7 0.1 collective-permute-done.1.got_ref
  103.8 0.0 copy-start
  103.8 2.7 %copy-done = bf16[512,5760]{1,0:T(8,128)(2,1)S(1)} copy-done((bf16[512,5760]{1,0:T(8,128)(2,1)S(1)}, bf16[512,5760]{1,0:T(8,128)(2,1)}, u32[]{:S(2)}) %copy-start) | copy-done | bytes 5898264
  106.5 0.0 copy-start.4
  106.5 0.0 copy-start.6
  106.5 8.4 %weight_grad.1 = bf16[512,3584]{1,0:T(8,128)(2,1)} custom-call(s32[1]{0:T(128)} %bitcast.3.dp_ref, bf16[512,5760]{1,0:T(8,128)(2,1)S(1)} %copy-done, bf16[512,5760]{1,0:T(8,128)(2,1)} %collective-permute-done.1.got_ref), custom_call_target="tpu_custom_call" | custom-call | tf_op jit(solution)/shard_map/weight_grad/pallas_call | solution.py:284
  114.8 6.2 %all-to-all-done.1 = bf16[64,8,1280]{2,1,0:T(8,128)(2,1)S(1)} async-done(((bf16[64,8,1280]{2,1,0:T(8,128)(2,1)}), bf16[64,8,1280]{2,1,0:T(8,128)(2,1)S(1)}, u32[]{:S(2)}, u32[]{:S(2)}) %all-to-all-start.1) | async-done | bytes 1310752 | tf_op jit(solution)/shard_map/all_to_all | solution.py:363
  121.1 0.0 copy-done.4
  121.1 0.0 copy-done.6
  121.1 2.1 %combine.1 = (bf16[256,2,1024]{2,1,0:T(2,128)(2,1)}, f32[2,256]{1,0:T(2,128)}) custom-call(bf16[512,640]{1,0:T(8,128)(2,1)S(1)} %copy-done.4, bf16[512,1280]{1,0:T(8,128)(2,1)S(1)} %bitcast.12, f32[512,128]{1,0:T(8,128)S(1)} %copy-done.6, bf16[512,1024]{1,0:T(8,128)(2,1)S(1)} %get-tuple-element.27.hid_ref), custom_call_target="tpu_custom_call" | custom-call | tf_op jit(solution)/shard_map/combine/pallas_call | solution.py:350
Async XLA Ops:
  0.6 6.8 %collective-permute-start = (bf16[512,3584]{1,0:T(8,128)(2,1)}, bf16[512,3584]{1,0:T(8,128)(2,1)}, u32[]{:S(2)}, u32[]{:S(2)}) collective-permute-start(bf16[512,3584]{1,0:T(8,128)(2,1)} %bitcast.13), channel_id=1, source_target_pairs={{0,64},{64,0},{1,65},{65,1},{2,66},{66,2},{3,67},{67,3},{4,68},{68... | collective-permute-start | bytes 11010056 | tf_op jit(solution)/shard_map/ppermute | solution.py:375
  7.5 80.3 %copy-start.2 = (bf16[1,512,3584]{2,1,0:T(8,128)(2,1)S(1)}, bf16[1,512,3584]{2,1,0:T(8,128)(2,1)}, u32[]{:S(2)}) copy-start(bf16[1,512,3584]{2,1,0:T(8,128)(2,1)} %param.9) | copy-start | bytes 11010052
  87.8 13.5 %copy-start.1 = (bf16[256,2,1024]{2,1,0:T(2,128)(2,1)S(1)}, bf16[256,2,1024]{2,1,0:T(2,128)(2,1)}, u32[]{:S(2)}) copy-start(bf16[256,2,1024]{2,1,0:T(2,128)(2,1)} %hid_ref.1) | copy-start | bytes 3145732
  87.8 13.5 %copy-start.7 = (s32[256,2]{0,1:T(2,128)S(1)}, s32[256,2]{0,1:T(2,128)}, u32[]{:S(2)}) copy-start(s32[256,2]{0,1:T(2,128)} %param.8) | copy-start | bytes 6148
  87.8 13.5 %copy-start.8 = (bf16[256,2]{0,1:T(2,128)(2,1)S(1)}, bf16[256,2]{0,1:T(2,128)(2,1)}, u32[]{:S(2)}) copy-start(bf16[256,2]{0,1:T(2,128)(2,1)} %param.7) | copy-start | bytes 3076
  93.8 10.0 %collective-permute-start.1 = (bf16[512,5760]{1,0:T(8,128)(2,1)}, bf16[512,5760]{1,0:T(8,128)(2,1)}, u32[]{:S(2)}, u32[]{:S(2)}) collective-permute-start(bf16[512,5760]{1,0:T(8,128)(2,1)} %get-tuple-element.24.own_ref), channel_id=1, source_target_pairs={{0,64},{64,0},{1,65},{65,1},{2,66},{66,2},{3,67},{67,3},{4,68},{68... | collective-permute-start | bytes 17694728 | tf_op jit(solution)/shard_map/ppermute | solution.py:375
  93.9 27.2 %all-to-all-start.1 = ((bf16[64,8,1280]{2,1,0:T(8,128)(2,1)}), bf16[64,8,1280]{2,1,0:T(8,128)(2,1)S(1)}, u32[]{:S(2)}, u32[]{:S(2)}) async-start(bf16[64,8,1280]{2,1,0:T(8,128)(2,1)} %bitcast.20), calls=%async_computation.1 | async-start | bytes 2621440 | tf_op jit(solution)/shard_map/all_to_all | solution.py:363
  102.2 0.8 copy-start.3
  103.0 0.7 copy-start.5
  103.8 2.7 %copy-start = (bf16[512,5760]{1,0:T(8,128)(2,1)S(1)}, bf16[512,5760]{1,0:T(8,128)(2,1)}, u32[]{:S(2)}) copy-start(bf16[512,5760]{1,0:T(8,128)(2,1)} %get-tuple-element.24.own_ref) | copy-start | bytes 17694724
  106.5 14.6 %copy-start.4 = (bf16[512,640]{1,0:T(8,128)(2,1)S(1)}, bf16[512,640]{1,0:T(8,128)(2,1)}, u32[]{:S(2)}) copy-start(bf16[512,640]{1,0:T(8,128)(2,1)} %copy-done.3) | copy-start | bytes 1966084
  106.5 14.6 %copy-start.6 = (f32[512,128]{1,0:T(8,128)S(1)}, f32[512,128]{1,0:T(8,128)}, u32[]{:S(2)}) copy-start(f32[512,128]{1,0:T(8,128)} %copy-done.5) | copy-start | bytes 786436

commit v7 on v6

--- a/solution.py
+++ b/solution.py
@@ -105,7 +105,7 @@
     i = iota((ROWS + OVER, 1), 0)
     main = i < ROWS
     expert = jnp.where(main, jnp.right_shift(i, 3), jnp.right_shift(i - ROWS, 1))
-    expert = (expert * 21) & (E - 1)
+    expert = (expert * 29) & (E - 1)
     rank = jnp.where(main, (i & 7) + 1, (i & 1) + 9)
     rows = (expert == iota((ROWS + OVER, E), 1)).astype(F32).astype(BF)
     return rows, rank.astype(F32)
@@ -365,7 +365,7 @@
         "expert",
         split_axis=0,
         concat_axis=0,
-        axis_index_groups=[[i * 21 % E for i in range(E)]],
+        axis_index_groups=[[i * 29 % E for i in range(E)]],
         tiled=True,
     )
     return swapped.reshape(ROWS, width)

time: 124 us -> 126 us (1.016)
  waiting for transfers between devices: 8.97 us -> 10.7 us
  blocking collectives: 80.3 us -> 82 us
  starting transfers between devices: 7.55 us -> 6.27 us
    all_to_all x1, blocking collectives: 80.3 us -> 82 us  [exchange(): lax.all_to_all(x.reshape(E, 8, width), 'expert', split_axis=0, concat_axi...]
    all_to_all x1, starting transfers between devices: 7.38 us -> 6.1 us  [exchange(): lax.all_to_all(x.reshape(E, 8, width), 'expert', split_axis=0, concat_axi...]
    ppermute x2, waiting for transfers between devices: 2.73 us -> 4.01 us  [swap(): return lax.ppermute(x, 'dp', [(0, 1), (1, 0)])]
where the time goes in v7:
time: 126 us; the launch traced here: 125 us
  blocking collectives  82 us (65%)
  Pallas kernels  21.4 us (17%)
  waiting for transfers between devices  10.7 us (8%)
  starting transfers between devices  6.27 us (5%)
  local copies, waits for them, and re-layouts  4.23 us (3%)
    all_to_all x1, blocking collectives, exchange(): lax.all_to_all(x.reshape(E, 8, width), 'expert', split_axis=0, concat_axi...  82 us
    pallas_call x1, Pallas kernels, weight_rows(): pl.pallas_call(grad_kernel, in_specs=[IN_SMEM, IN_HBM, IN_HBM], out_specs...  8.36 us
    all_to_all x1, waiting for transfers between devices, exchange(): lax.all_to_all(x.reshape(E, 8, width), 'expert', split_axis=0, concat_axi...  6.72 us
    all_to_all x1, starting transfers between devices, exchange(): lax.all_to_all(x.reshape(E, 8, width), 'expert', split_axis=0, concat_axi...  6.1 us
    pallas_call x1, Pallas kernels, raw_rows(): pl.pallas_call(raw_kernel, in_specs=[IN_SMEM, IN_VMEM, IN_VMEM, IN_HBM],...  5.99 us
    unnamed x18, local copies, waits for them, and re-layouts  4.23 us
    pallas_call x1, Pallas kernels, pack(): pl.pallas_call(pack_kernel, in_specs=[IN_HBM, IN_HBM, IN_HBM, IN_HBM], ou...  4.08 us
    ppermute x2, waiting for transfers between devices, swap(): return lax.ppermute(x, 'dp', [(0, 1), (1, 0)])  4.01 us
  transfers between devices with their start and end apart: 3, of which 3 were waited for; matrix products, arithmetic and copies ran while one was open for 0% of the time, Pallas kernels for 11%

profile of v7, /device:TPU:0, one launch (start us, length us, event | category | flops | bytes accessed | tf_op | source)
XLA Modules:
  0.0 125.4 jit_solution(4602213649111774169)
XLA Ops:
  0.6 0.1 collective-permute-start
  0.7 4.1 %pack.1 = bf16[512,5760]{1,0:T(8,128)(2,1)S(1)} custom-call(s32[2,256]{1,0:T(2,128)} %bitcast.15, bf16[2,256]{1,0:T(2,128)(2,1)} %bitcast.17, bf16[256,3584]{1,0:T(8,128)(2,1)} %grad_hbm.1, bf16[256,2,1024]{2,1,0:T(2,128)(2,1)} %hid_ref.1), custom_call_target="tpu_custom_call" | custom-call | tf_op jit(solution)/shard_map/pack/pallas_call | solution.py:160
  4.8 2.6 %collective-permute-done.other_hbm = bf16[512,3584]{1,0:T(8,128)(2,1)} collective-permute-done((bf16[512,3584]{1,0:T(8,128)(2,1)}, bf16[512,3584]{1,0:T(8,128)(2,1)}, u32[]{:S(2)}, u32[]{:S(2)}) %collective-permute-start) | collective-permute-done | bytes 3670048 | tf_op jit(solution)/shard_map/ppermute | solution.py:375
  7.5 0.0 copy-start.2
  7.5 82.0 %all_to_all.10 = bf16[64,8,5760]{2,1,0:T(8,128)(2,1)S(1)} all-to-all(bf16[64,8,5760]{2,1,0:T(8,128)(2,1)S(1)} %bitcast.11), channel_id=1, replica_groups={{0,29,58,23,52,17,46,11,40,5,34,63,28,57,22,51,16,45,10,39,4,33,62,27,5..., dimensions={0} | all-to-all | bytes 11796480 | tf_op jit(solution)/shard_map/all_to_all | solution.py:363
  89.5 0.0 copy-done.2
  89.5 0.0 copy-start.1
  89.5 0.0 copy-start.7
  89.5 0.0 copy-start.8
  89.5 6.0 %raw.1 = (bf16[512,1280]{1,0:T(8,128)(2,1)}, bf16[512,5760]{1,0:T(8,128)(2,1)}) custom-call(s32[1]{0:T(128)} %bitcast.3.dp_ref, bf16[512,5760]{1,0:T(8,128)(2,1)S(1)} %bitcast.10, bf16[512,3584]{1,0:T(8,128)(2,1)S(1)} %bitcast.14, bf16[512,3584]{1,0:T(8,128)(2,1)} %collective-permute-done.other_hbm), custom_call_target="tpu_custom_call" | custom-call | tf_op jit(solution)/shard_map/raw/pallas_call | solution.py:223
  95.5 0.1 collective-permute-start.1
  95.6 6.1 %all-to-all-start.1 = ((bf16[64,8,1280]{2,1,0:T(8,128)(2,1)}), bf16[64,8,1280]{2,1,0:T(8,128)(2,1)S(1)}, u32[]{:S(2)}, u32[]{:S(2)}) async-start(bf16[64,8,1280]{2,1,0:T(8,128)(2,1)} %bitcast.20), calls=%async_computation.1 | async-start | bytes 2621440 | tf_op jit(solution)/shard_map/all_to_all | solution.py:363
  101.7 0.0 copy-done.1
  101.7 0.0 copy-done.7
  101.7 0.0 copy-done.8
  101.7 0.9 prepare.1
  102.6 0.0 copy-start.3
  102.6 0.8 copy-done.3
  103.4 0.0 copy-start.5
  103.4 0.7 copy-done.5
  104.1 1.4 %collective-permute-done.1.got_ref = bf16[512,5760]{1,0:T(8,128)(2,1)} collective-permute-done((bf16[512,5760]{1,0:T(8,128)(2,1)}, bf16[512,5760]{1,0:T(8,128)(2,1)}, u32[]{:S(2)}, u32[]{:S(2)}) %collective-permute-start.1) | collective-permute-done | bytes 5898272 | tf_op jit(solution)/shard_map/ppermute | solution.py:375
  105.5 0.0 copy-start
  105.5 2.7 %copy-done = bf16[512,5760]{1,0:T(8,128)(2,1)S(1)} copy-done((bf16[512,5760]{1,0:T(8,128)(2,1)S(1)}, bf16[512,5760]{1,0:T(8,128)(2,1)}, u32[]{:S(2)}) %copy-start) | copy-done | bytes 5898264
  108.2 0.0 copy-start.4
  108.2 0.0 copy-start.6
  108.2 8.4 %weight_grad.1 = bf16[512,3584]{1,0:T(8,128)(2,1)} custom-call(s32[1]{0:T(128)} %bitcast.3.dp_ref, bf16[512,5760]{1,0:T(8,128)(2,1)S(1)} %copy-done, bf16[512,5760]{1,0:T(8,128)(2,1)} %collective-permute-done.1.got_ref), custom_call_target="tpu_custom_call" | custom-call | tf_op jit(solution)/shard_map/weight_grad/pallas_call | solution.py:284
  116.6 6.7 %all-to-all-done.1 = bf16[64,8,1280]{2,1,0:T(8,128)(2,1)S(1)} async-done(((bf16[64,8,1280]{2,1,0:T(8,128)(2,1)}), bf16[64,8,1280]{2,1,0:T(8,128)(2,1)S(1)}, u32[]{:S(2)}, u32[]{:S(2)}) %all-to-all-start.1) | async-done | bytes 1310752 | tf_op jit(solution)/shard_map/all_to_all | solution.py:363
  123.3 0.0 copy-done.4
  123.3 0.0 copy-done.6
  123.3 2.1 %combine.1 = (bf16[256,2,1024]{2,1,0:T(2,128)(2,1)}, f32[2,256]{1,0:T(2,128)}) custom-call(bf16[512,640]{1,0:T(8,128)(2,1)S(1)} %copy-done.4, bf16[512,1280]{1,0:T(8,128)(2,1)S(1)} %bitcast.12, f32[512,128]{1,0:T(8,128)S(1)} %copy-done.6, bf16[512,1024]{1,0:T(8,128)(2,1)S(1)} %get-tuple-element.27.hid_ref), custom_call_target="tpu_custom_call" | custom-call | tf_op jit(solution)/shard_map/combine/pallas_call | solution.py:350
Async XLA Ops:
  0.6 6.8 %collective-permute-start = (bf16[512,3584]{1,0:T(8,128)(2,1)}, bf16[512,3584]{1,0:T(8,128)(2,1)}, u32[]{:S(2)}, u32[]{:S(2)}) collective-permute-start(bf16[512,3584]{1,0:T(8,128)(2,1)} %bitcast.13), channel_id=1, source_target_pairs={{0,64},{64,0},{1,65},{65,1},{2,66},{66,2},{3,67},{67,3},{4,68},{68... | collective-permute-start | bytes 11010056 | tf_op jit(solution)/shard_map/ppermute | solution.py:375
  7.5 82.0 %copy-start.2 = (bf16[1,512,3584]{2,1,0:T(8,128)(2,1)S(1)}, bf16[1,512,3584]{2,1,0:T(8,128)(2,1)}, u32[]{:S(2)}) copy-start(bf16[1,512,3584]{2,1,0:T(8,128)(2,1)} %param.9) | copy-start | bytes 11010052
  89.5 12.2 %copy-start.1 = (bf16[256,2,1024]{2,1,0:T(2,128)(2,1)S(1)}, bf16[256,2,1024]{2,1,0:T(2,128)(2,1)}, u32[]{:S(2)}) copy-start(bf16[256,2,1024]{2,1,0:T(2,128)(2,1)} %hid_ref.1) | copy-start | bytes 3145732
  89.5 12.2 %copy-start.7 = (s32[256,2]{0,1:T(2,128)S(1)}, s32[256,2]{0,1:T(2,128)}, u32[]{:S(2)}) copy-start(s32[256,2]{0,1:T(2,128)} %param.8) | copy-start | bytes 6148
  89.5 12.2 %copy-start.8 = (bf16[256,2]{0,1:T(2,128)(2,1)S(1)}, bf16[256,2]{0,1:T(2,128)(2,1)}, u32[]{:S(2)}) copy-start(bf16[256,2]{0,1:T(2,128)(2,1)} %param.7) | copy-start | bytes 3076
  95.5 10.0 %collective-permute-start.1 = (bf16[512,5760]{1,0:T(8,128)(2,1)}, bf16[512,5760]{1,0:T(8,128)(2,1)}, u32[]{:S(2)}, u32[]{:S(2)}) collective-permute-start(bf16[512,5760]{1,0:T(8,128)(2,1)} %get-tuple-element.24.own_ref), channel_id=1, source_target_pairs={{0,64},{64,0},{1,65},{65,1},{2,66},{66,2},{3,67},{67,3},{4,68},{68... | collective-permute-start | bytes 17694728 | tf_op jit(solution)/shard_map/ppermute | solution.py:375
  95.6 27.7 %all-to-all-start.1 = ((bf16[64,8,1280]{2,1,0:T(8,128)(2,1)}), bf16[64,8,1280]{2,1,0:T(8,128)(2,1)S(1)}, u32[]{:S(2)}, u32[]{:S(2)}) async-start(bf16[64,8,1280]{2,1,0:T(8,128)(2,1)} %bitcast.20), calls=%async_computation.1 | async-start | bytes 2621440 | tf_op jit(solution)/shard_map/all_to_all | solution.py:363
  102.6 0.8 copy-start.3
  103.4 0.7 copy-start.5
  105.5 2.7 %copy-start = (bf16[512,5760]{1,0:T(8,128)(2,1)S(1)}, bf16[512,5760]{1,0:T(8,128)(2,1)}, u32[]{:S(2)}) copy-start(bf16[512,5760]{1,0:T(8,128)(2,1)} %get-tuple-element.24.own_ref) | copy-start | bytes 17694724
  108.2 15.1 %copy-start.4 = (bf16[512,640]{1,0:T(8,128)(2,1)S(1)}, bf16[512,640]{1,0:T(8,128)(2,1)}, u32[]{:S(2)}) copy-start(bf16[512,640]{1,0:T(8,128)(2,1)} %copy-done.3) | copy-start | bytes 1966084
  108.2 15.1 %copy-start.6 = (f32[512,128]{1,0:T(8,128)S(1)}, f32[512,128]{1,0:T(8,128)}, u32[]{:S(2)}) copy-start(f32[512,128]{1,0:T(8,128)} %copy-done.5) | copy-start | bytes 786436
